TPU v7x, 32 devices: a whole 2x2x4 slice. The times are simulated.
32 devices in a mesh: dp: 8 (over y, x, core), tensor: 4 (over z).
Axes of the slice: x: 2, y: 2, z: 4, core: 2. Of those that a mesh axis runs over, the one named last changes fastest.
Arguments:
- tokens: bfloat16 [6144, 2048], P('dp'), may hold values from -6 to 6
- targets: bfloat16 [6144, 2048], P('dp'), may hold values from -6 to 6
- up_weight: bfloat16 [8, 64, 256, 256], P('dp', 'tensor'), may hold values from -6 to 6
- down_weight: bfloat16 [8, 64, 256, 256], P('dp', 'tensor'), may hold values from -6 to 6
- block_rows: int32 [64], P('tensor'), may hold values from 0 to 7, as said below
- block_columns: int32 [64], P('tensor'), may hold values from 0 to 7, as said below
Outputs:
- new_up: bfloat16 [8, 64, 256, 256], P('dp', 'tensor')
- new_down: bfloat16 [8, 64, 256, 256], P('dp', 'tensor')
- input_grad: bfloat16 [6144, 2048], P('dp', 'tensor')
Inputs may be any that keep to these rules, and one draw needn't show every extreme that they name: Within each tensor shard the 16 blocks sit at distinct (block_rows, block_columns) positions, and every hidden block of a shard holds exactly 2 of them; up_weight and down_weight share this pattern. `block_columns`: hidden block indices within a shard.
All inputs are finite; a program needn't handle non-finite values.
Results may differ from a plain program's by a relative error of at most 0.015.
Values may be sent and summed in bfloat16 or wider, within the bound.
No kernel may reach another device: no remote copies, remote signals or barrier semaphores. Data moves between devices by JAX's collectives and lax.ppermute only.
A program may use at most 128 MiB of HBM per device.

v0:
```python
import jax
import jax.numpy as jnp
from jax import lax
from jax.sharding import PartitionSpec as P

D = 2048
H = 8192


step_rate = 0.5


def from_partner(x, axis, apart):
    return lax.ppermute(x, axis, [(i, i ^ 1 << apart) for i in range(lax.axis_size(axis))])


def on_device(tokens, targets, up_weight, down_weight, block_rows, block_columns):
    tok_count = tokens.shape[0]
    width = tokens.shape[1]
    block_size = up_weight.shape[2]
    model_blocks = width // block_size
    tensor_count = lax.axis_size("tensor")
    shard_hidden = H // (tensor_count * block_size)
    level = (lax.axis_size("dp").bit_length() - 1) // 2
    scale_in = (D // 4) ** (-0.5)
    scale_out = (H // 4) ** (-0.5)
    up_local = up_weight[0]
    down_local = down_weight[0]
    peer_up, peer_down = from_partner((up_local, down_local), "dp", level)
    col_select = (block_columns[:, None] == jnp.arange(shard_hidden)[None, :]).astype(jnp.float32)
    row_select = (block_rows[:, None] == jnp.arange(model_blocks)[None, :]).astype(jnp.float32)
    tok_blocks = jnp.take(tokens.reshape(tok_count, model_blocks, block_size), block_rows, axis=1)
    first = jnp.einsum("tnk,nkj->tnj", tok_blocks, up_local, preferred_element_type=jnp.float32)
    hidden_pre = (
        jnp.einsum("tnj,nh->thj", first, col_select, precision=lax.Precision.HIGHEST) * scale_in
    )
    active = jax.nn.silu(hidden_pre).astype(jnp.bfloat16)
    active_blocks = jnp.take(active, block_columns, axis=1)
    second = jnp.einsum(
        "tnj,njk->tnk", active_blocks, down_local, preferred_element_type=jnp.float32
    )
    out_part = (
        jnp.einsum("tnk,nd->tdk", second, row_select, precision=lax.Precision.HIGHEST) * scale_out
    )
    out_part = out_part.reshape(tok_count, width).astype(jnp.bfloat16)
    output_total = lax.psum(out_part, "tensor").astype(jnp.float32)
    error_full = (output_total - targets.astype(jnp.float32)).astype(jnp.bfloat16)
    error_blocks = jnp.take(
        error_full.reshape(tok_count, model_blocks, block_size), block_rows, axis=1
    )
    grad_down = scale_out * jnp.einsum(
        "tnj,tnk->njk", active_blocks, error_blocks, preferred_element_type=jnp.float32
    )
    dact_blocks = jnp.einsum(
        "tnk,njk->tnj", error_blocks, down_local, preferred_element_type=jnp.float32
    )
    dact = (
        jnp.einsum("tnj,nh->thj", dact_blocks, col_select, precision=lax.Precision.HIGHEST)
        * scale_out
    )
    sigma = jax.nn.sigmoid(hidden_pre)
    dpre = (dact * sigma * (1.0 + hidden_pre * (1.0 - sigma))).astype(jnp.bfloat16)
    dpre_blocks = jnp.take(dpre, block_columns, axis=1)
    grad_up = scale_in * jnp.einsum(
        "tnk,tnj->nkj", tok_blocks, dpre_blocks, preferred_element_type=jnp.float32
    )
    back_blocks = jnp.einsum(
        "tnj,nkj->tnk", dpre_blocks, up_local, preferred_element_type=jnp.float32
    )
    back_part = (
        jnp.einsum("tnk,nd->tdk", back_blocks, row_select, precision=lax.Precision.HIGHEST)
        * scale_in
    )
    back_part = back_part.reshape(tok_count, width).astype(jnp.bfloat16)
    grad_sum = lax.psum_scatter(back_part, "tensor", scatter_dimension=1, tiled=True).astype(
        jnp.float32
    )
    input_grad = grad_sum.astype(jnp.bfloat16)
    new_up = (
        0.5 * (up_local.astype(jnp.float32) + peer_up.astype(jnp.float32)) - step_rate * grad_up
    ).astype(jnp.bfloat16)
    new_down = (
        0.5 * (down_local.astype(jnp.float32) + peer_down.astype(jnp.float32))
        - step_rate * grad_down
    ).astype(jnp.bfloat16)
    return (new_up[None], new_down[None], input_grad)


def solution(mesh):
    return jax.shard_map(
        on_device,
        mesh=mesh,
        in_specs=(
            P("dp", None),
            P("dp", None),
            P("dp", "tensor", None, None),
            P("dp", "tensor", None, None),
            P("tensor"),
            P("tensor"),
        ),
        out_specs=(P("dp", "tensor", None, None), P("dp", "tensor", None, None), P("dp", "tensor")),
        check_vma=False,
    )
```

profile of v0, /device:TPU:0, one launch (start us, length us, event | category | flops | bytes accessed | tf_op | source)
XLA Modules:
  0.0 357.7 jit_solution(6178012861275461312)
XLA Ops:
  7.2 0.0 all-reduce.2.cloned.1.call-start
  7.2 0.7 compare_select_fusion.1
  7.9 0.7 compare_and_fusion
  8.5 0.7 compare_select_fusion
  9.2 4.6 %copy.15 = bf16[768,2048]{0,1:T(8,128)(2,1)} copy(bf16[768,2048]{1,0:T(8,128)(2,1)} %param.8) | data formatting | bytes 6291456 | tf_op args[0]
  13.9 3.2 copy.16
  17.0 3.6 %gather_fusion = bf16[16,768,256]{2,1,0:T(8,128)(2,1)} fusion(bf16[768,8,256]{2,0,1:T(8,128)(2,1)S(1)} %copy.16, s32[1024]{0:T(1024)S(1)} %pad_clamp_fusion.1), kind=kCustom, calls=%fused_computation.clone | custom fusion | bytes 12582976 | tf_op jit(solution)/shard_map/jit(_take)/gather | solution.py:32
  20.6 0.0 copy-start.1
  20.6 5.3 %fusion.29 = f32[768,16,256]{2,0,1:T(8,128)S(1)} fusion(bf16[16,768,256]{2,1,0:T(8,128)(2,1)} %gather_fusion, pred[16]{0:T(512)(128)(4,1)S(1)} %get-tuple-element.7, bf16[1,16,256,256]{3,2,1,0:T(8,128)(2,1)} %param.10), kind=kOutput, calls=%fused_computation.44 | convolution fusion | flops 1613758464 | bytes 20971536 | tf_op jit(solution)/shard_map/tnk,nkj->tnj/dot_general | solution.py:33
  25.9 0.0 copy-done.1
  25.9 12.7 %fusion.24 = (bf16[768,8,256]{2,1,0:T(8,128)(2,1)S(1)}, f32[8,768,256]{2,0,1:T(8,128)}) fusion(f32[768,16,256]{2,0,1:T(8,128)S(1)} %fusion.29, s32[16]{0:T(128)S(1)} %copy-done.1), kind=kOutput, calls=%fused_computation.32 | convolution fusion | flops 311427200 | bytes 22020160 | tf_op jit(solution)/shard_map/tnj,nh->thj/dot_general | solution.py:35
  38.6 0.6 copy.18
  39.3 3.6 %gather_fusion.1 = bf16[16,768,256]{2,1,0:T(8,128)(2,1)} fusion(bf16[768,8,256]{2,0,1:T(8,128)(2,1)S(1)} %copy.18, s32[1024]{0:T(1024)S(1)} %pad_clamp_fusion), kind=kCustom, calls=%fused_computation.1.clone | custom fusion | bytes 12582976 | tf_op jit(solution)/shard_map/jit(_take)/gather | solution.py:38
  42.9 0.0 copy-start
  42.9 5.3 %fusion.32 = f32[768,16,256]{2,0,1:T(8,128)S(1)} fusion(bf16[16,768,256]{2,1,0:T(8,128)(2,1)} %gather_fusion.1, pred[16]{0:T(512)(128)(4,1)S(1)} %get-tuple-element.6, bf16[1,16,256,256]{3,2,1,0:T(8,128)(2,1)} %param.11), kind=kOutput, calls=%fused_computation.45 | convolution fusion | flops 1613758464 | bytes 20971536 | tf_op jit(solution)/shard_map/tnj,njk->tnk/dot_general | solution.py:39
  48.2 0.0 copy-done
  48.2 20.9 %fusion.41 = bf16[768,8,256]{2,1,0:T(8,128)(2,1)S(1)} fusion(f32[768,16,256]{2,0,1:T(8,128)S(1)} %fusion.32, s32[16]{0:T(128)S(1)} %copy-done), kind=kOutput, calls=%fused_computation.50 | convolution fusion | flops 305135744 | bytes 15728704 | tf_op jit(solution)/shard_map/tnk,nd->tdk/dot_general | solution.py:43
  69.1 3.6 %copy.30 = bf16[768,8,256]{0,2,1:T(8,128)(2,1)} copy(bf16[768,8,256]{2,1,0:T(8,128)(2,1)S(1)} %fusion.41) | data formatting | bytes 6291456 | tf_op jit(solution)/shard_map/convert_element_type | solution.py:45
  72.7 0.0 all-reduce.2.cloned.1.call-update
  72.7 0.0 reduce-scatter.2.cloned.1.call-start
  72.8 3.2 copy.21
  75.9 120.7 %all-reduce.2.cloned.1.call-done = bf16[768,2048]{0,1:T(8,128)(2,1)} async-done(((bf16[768,2048]{0,1:T(8,128)(2,1)}), bf16[768,2048]{0,1:T(8,128)(2,1)}) %all-reduce.2.cloned.1.call-update) | async-done | bytes 3145744 | tf_op jit(solution)/shard_map/psum | solution.py:46
  196.6 4.3 %subtract_convert_fusion = bf16[768,2048]{0,1:T(8,128)(2,1)} fusion(bf16[768,2048]{0,1:T(8,128)(2,1)S(1)} %copy.21, bf16[768,2048]{0,1:T(8,128)(2,1)} %all-reduce.2.cloned.1.call-done), kind=kLoop, calls=%fused_computation.38 | loop fusion | flops 6291456 | bytes 9437184 | tf_op jit(solution)/shard_map/convert_element_type | solution.py:47
  201.0 3.2 copy.22
  204.1 3.5 gather_fusion.2
  207.7 5.3 %fusion.35 = f32[768,16,256]{2,0,1:T(8,128)S(1)} fusion(bf16[16,768,256]{2,1,0:T(8,128)(2,1)} %gather_fusion.2, pred[16]{0:T(512)(128)(4,1)S(1)} %get-tuple-element.7, bf16[1,16,256,256]{3,2,1,0:T(8,128)(2,1)} %param.11), kind=kOutput, calls=%fused_computation.46 | convolution fusion | flops 1613758464 | bytes 20971536 | tf_op jit(solution)/shard_map/tnk,njk->tnj/dot_general | solution.py:54
  213.0 14.1 %fusion.13 = bf16[768,8,256]{2,1,0:T(8,128)(2,1)S(1)} fusion(f32[8,768,256]{2,0,1:T(8,128)} %get-tuple-element.5, f32[768,16,256]{2,0,1:T(8,128)S(1)} %fusion.35, s32[16]{0:T(128)S(1)} %copy-done.1), kind=kOutput, calls=%fused_computation.18 | convolution fusion | flops 319291520 | bytes 22020160 | tf_op jit(solution)/shard_map/tnj,nh->thj/dot_general | solution.py:58
  227.0 0.6 copy.24
  227.7 3.5 gather_fusion.3
  231.2 5.3 %fusion.38 = f32[768,16,256]{2,0,1:T(8,128)S(1)} fusion(bf16[16,768,256]{2,1,0:T(8,128)(2,1)} %gather_fusion.3, pred[16]{0:T(512)(128)(4,1)S(1)} %get-tuple-element.6, bf16[1,16,256,256]{3,2,1,0:T(8,128)(2,1)} %param.10), kind=kOutput, calls=%fused_computation.47 | convolution fusion | flops 1613758464 | bytes 20971536 | tf_op jit(solution)/shard_map/tnj,nkj->tnk/dot_general | solution.py:67
  236.5 10.1 %multiply_convert_fusion = bf16[8,768,256]{2,0,1:T(8,128)(2,1)S(1)} fusion(f32[768,16,256]{2,0,1:T(8,128)S(1)} %fusion.38, s32[16]{0:T(128)S(1)} %copy-done), kind=kOutput, calls=%fused_computation.37 | convolution fusion | flops 305135744 | bytes 15728704 | tf_op jit(solution)/shard_map/tnk,nd->tdk/dot_general | solution.py:71
  246.6 2.8 copy.31
  249.4 0.0 reduce-scatter.2.cloned.1.call-update
  249.4 1.5 collective-permute-start
  250.9 0.0 slice-start
  250.9 0.0 slice-start.1
  250.9 0.6 collective-permute-start.1
  251.5 46.8 %collective-permute-done = bf16[16,256,256]{2,1,0:T(8,128)(2,1)} collective-permute-done((bf16[16,256,256]{2,1,0:T(8,128)(2,1)}, bf16[16,256,256]{2,1,0:T(8,128)(2,1)}, u32[]{:S(2)}, u32[]{:S(2)}) %collective-permute-start) | collective-permute-done | bytes 2097184 | tf_op jit(solution)/shard_map/ppermute | solution.py:14
  298.3 10.0 %fusion.48 = bf16[1,16,256,256]{3,2,1,0:T(8,128)(2,1)} fusion(bf16[16,256,256]{2,1,0:T(8,128)(2,1)} %collective-permute-done, bf16[16,768,256]{2,1,0:T(8,128)(2,1)} %gather_fusion.3, pred[16]{0:T(512)(128)(4,1)S(1)} %get-tuple-element.6, bf16[16,768,256]{2,1,0:T(8,128)(2,1)} %gather_fusion, pred[16]{0:T(512)(128)(4,1)S(1)} %get-tuple-element.7, ...), kind=kOutput, calls=%fused_computation.51 | convolution fusion | flops 1624244224 | bytes 18874400 | tf_op jit(solution)/shard_map/tnk,tnj->nkj/dot_general | solution.py:64
  308.3 33.8 %collective-permute-done.1 = bf16[16,256,256]{2,1,0:T(8,128)(2,1)} collective-permute-done((bf16[16,256,256]{2,1,0:T(8,128)(2,1)}, bf16[16,256,256]{2,1,0:T(8,128)(2,1)}, u32[]{:S(2)}, u32[]{:S(2)}) %collective-permute-start.1) | collective-permute-done | bytes 2097184 | tf_op jit(solution)/shard_map/ppermute | solution.py:14
  342.0 0.0 slice-done
  342.0 0.0 slice-done.1
  342.0 8.4 %fusion.49 = bf16[1,16,256,256]{3,2,1,0:T(8,128)(2,1)} fusion(bf16[16,256,256]{2,1,0:T(8,128)(2,1)} %collective-permute-done.1, bf16[16,768,256]{2,1,0:T(8,128)(2,1)} %gather_fusion.2, pred[16]{0:T(512)(128)(4,1)S(1)} %get-tuple-element.7, bf16[16,768,256]{2,1,0:T(8,128)(2,1)S(1)} %bitcast.105, pred[16]{0:T(512)(128)(4,1)S(1)} %get-tuple-element.6, ...), kind=kOutput, calls=%fused_computation.52 | convolution fusion | flops 1624244224 | bytes 18874400 | tf_op jit(solution)/shard_map/tnj,tnk->njk/dot_general | solution.py:51
  350.5 0.0 reduce-scatter.2.cloned.1.call-done
  (3 shorter events, 0.0 us)
Async XLA Ops:
  7.2 189.5 %all-reduce.2.cloned.1.call-start = ((), (), s32[]{:S(2)}) async-start(), calls=%async_computation.1 | async-start | bytes 6291456 | tf_op jit(solution)/shard_map/psum | solution.py:46
  20.6 5.3 %copy-start.1 = (s32[16]{0:T(128)S(1)}, s32[16]{0:T(128)}, u32[]{:S(2)}) copy-start(s32[16]{0:T(128)} %param.13) | copy-start | bytes 196
  42.9 5.3 %copy-start = (s32[16]{0:T(128)S(1)}, s32[16]{0:T(128)}, u32[]{:S(2)}) copy-start(s32[16]{0:T(128)} %param.12) | copy-start | bytes 196
  72.7 277.8 %reduce-scatter.2.cloned.1.call-start = ((), (), s32[]{:S(2)}) async-start(), calls=%async_computation.2 | async-start | bytes 3932160 | tf_op jit(solution)/shard_map/reduce_scatter | solution.py:75
  249.4 48.9 %collective-permute-start = (bf16[16,256,256]{2,1,0:T(8,128)(2,1)}, bf16[16,256,256]{2,1,0:T(8,128)(2,1)}, u32[]{:S(2)}, u32[]{:S(2)}) collective-permute-start(bf16[16,256,256]{2,1,0:T(8,128)(2,1)} %bitcast), channel_id=1, source_target_pairs={{0,8},{4,12},{8,0},{12,4},{16,24},{20,28},{24,16},{28,20},{1,9},{5... | collective-permute-start | bytes 6291464 | tf_op jit(solution)/shard_map/ppermute | solution.py:14
  250.9 91.1 %slice-start = ((s8[6291456]{0:T(1024)(128)(4,1)}), s8[4194304]{0:T(1024)(128)(4,1)S(1)}, s32[]{:S(2)}) async-start(s8[6291456]{0:T(1024)(128)(4,1)} %bitcast.104), calls=%async_computation.3 | async-start | bytes 8388608
  250.9 91.1 %slice-start.1 = ((s8[6291456]{0:T(1024)(128)(4,1)}), s8[2097152]{0:T(1024)(128)(4,1)S(1)}, s32[]{:S(2)}) async-start(s8[6291456]{0:T(1024)(128)(4,1)} %bitcast.104), calls=%async_computation.4 | async-start | bytes 4194304
  250.9 91.1 %collective-permute-start.1 = (bf16[16,256,256]{2,1,0:T(8,128)(2,1)}, bf16[16,256,256]{2,1,0:T(8,128)(2,1)}, u32[]{:S(2)}, u32[]{:S(2)}) collective-permute-start(bf16[16,256,256]{2,1,0:T(8,128)(2,1)} %bitcast.111), channel_id=1, source_target_pairs={{0,8},{4,12},{8,0},{12,4},{16,24},{20,28},{24,16},{28,20},{1,9},{5... | collective-permute-start | bytes 6291464 | tf_op jit(solution)/shard_map/ppermute | solution.py:14
Sparse Core Ops, SparseCore 0:
  72.8 123.7 all-reduce.1
  249.5 59.2 reduce-scatter.1
where the time goes:
time: 361 us; the launch traced here: 358 us
  waiting for transfers between devices  201 us (56%)
  matrix products  97.2 us (27%)
  local copies, waits for them, and re-layouts  36.2 us (10%)
  between operations  14.6 us (4%)
  other arithmetic  6.34 us (2%)
    psum x1, waiting for transfers between devices, on_device(): output_total = lax.psum(out_part, 'tensor').astype(jnp.float32)  121 us
    ppermute x2, waiting for transfers between devices, from_partner(): lax.ppermute(x, axis, [(i, i ^ 1 << apart) for i in range(lax.axis_size(a...  80.6 us
    dot_general x1, matrix products, on_device(): jnp.einsum('tnk,nd->tdk', second, row_select, precision=lax.Precision.HIG...  20.9 us
    dot_general x1, matrix products, on_device(): jnp.einsum('tnj,nh->thj', dact_blocks, col_select, precision=lax.Precisio...  14.1 us
    dot_general x1, matrix products, on_device(): jnp.einsum('tnj,nh->thj', first, col_select, precision=lax.Precision.HIGH...  12.7 us
    unnamed x11, local copies, waits for them, and re-layouts  10.6 us
    dot_general x1, matrix products, on_device(): jnp.einsum('tnk,nd->tdk', back_blocks, row_select, precision=lax.Precisio...  10.1 us
    dot_general x1, matrix products, on_device(): jnp.einsum('tnk,tnj->nkj', tok_blocks, dpre_blocks, preferred_element_typ...  9.98 us
  transfers between devices with their start and end apart: 4, of which 3 were waited for; matrix products, arithmetic and copies ran while one was open for 6% of the time, Pallas kernels for 0%

commit v1 on v0

v1 whole, which is shorter than its diff:
```python
import functools

import jax
import jax.numpy as jnp
from jax import lax
from jax.experimental import pallas as pl
from jax.experimental.pallas import tpu as pltpu
from jax.sharding import PartitionSpec as P

step_rate = 0.5
per_column = 2
ANY = pl.BlockSpec(memory_space=pltpu.HBM)
ANYV = pl.BlockSpec(memory_space=pltpu.VMEM)
SMEM = pl.BlockSpec(memory_space=pltpu.SMEM)
f32 = jnp.float32
bf16 = jnp.bfloat16
NT = (((1,), (1,)), ((), ()))
TN = (((0,), (0,)), ((), ()))


def params(mib=20):
    return pltpu.CompilerParams(vmem_limit_bytes=mib << 20)


def cost(flops, nbytes):
    return pl.CostEstimate(flops=1, bytes_accessed=1, transcendentals=0)


def lanes(index, size):
    return pl.ds(pl.multiple_of(index * size, size), size)


def column_table(cols_ref, table, count, blocks):
    for h in range(blocks // per_column):
        count[h] = 0
    for k in range(blocks):
        h = cols_ref[k]
        seen = count[h]
        table[per_column * h + seen] = k
        count[h] = seen + 1


def forward_kernel(start, scale_in, scale_out, direct, first, rows_ref, cols_ref, tok_hbm, up, down, dep, also, *refs):
    if first:
        up_hbm, down_hbm = up, down
        (part, act, fac, up, down), refs = refs[:5], refs[5:]
    else:
        (part, act, fac), refs = refs[2:5], refs[5:]
    outs, token, (tok, acc, table, count, sems), refs = refs[:direct], refs[direct], refs[direct + 1:direct + 6], refs[direct + 6:]
    size, width = tok.shape
    blocks, blk = up.shape[0], up.shape[1]
    mine = pl.ds(start, size)
    copies = [pltpu.make_async_copy(tok_hbm.at[mine], tok, sems.at[0])]
    if first:
        small = [pltpu.make_async_copy(rows_ref, refs[0], sems.at[1]), pltpu.make_async_copy(cols_ref, refs[1], sems.at[2])]
        rows_ref, cols_ref = refs
        copies += small
    for c in copies:
        c.start()
    if first:
        ups = [pltpu.make_async_copy(up_hbm.at[k], up.at[k], sems.at[3]) for k in range(blocks)]
        downs = [pltpu.make_async_copy(down_hbm.at[k], down.at[k], sems.at[4]) for k in range(blocks)]
        for c in ups + downs:
            c.start()
    acc[...] = jnp.zeros_like(acc)
    for c in copies[1:]:
        c.wait()
    column_table(cols_ref, table, count, blocks)
    copies[0].wait()
    if first:
        for c in ups:
            c.wait()
    for h in range(blocks // per_column):
        pre = None
        for j in range(per_column):
            k = table[per_column * h + j]
            term = jnp.dot(tok[:, lanes(rows_ref[k], blk)], up[k], preferred_element_type=f32)
            pre = term if pre is None else pre + term
        pre = pre * scale_in
        sig = 1.0 / (1.0 + jnp.exp(-pre))
        act[mine, h * blk:(h + 1) * blk] = (pre * sig).astype(bf16)
        fac[mine, h * blk:(h + 1) * blk] = (sig * (1.0 + pre * (1.0 - sig)) * scale_out).astype(bf16)
    if first:
        for c in downs:
            c.wait()
    for k in range(blocks):
        r = rows_ref[k]
        acc[r] += jnp.dot(act[mine, lanes(cols_ref[k], blk)], down[k], preferred_element_type=f32)
    for b in range(acc.shape[0]):
        part[:, b * blk:(b + 1) * blk] = (acc[b] * scale_out).astype(bf16)
    for c in shares_of(part, outs, sems.at[5]):
        c.wait()


def shares_of(whole, outs, sem):
    if not outs:
        return []
    share = whole.shape[1] // (len(outs) + 1)
    place = lax.axis_index("tensor")
    copies = [pltpu.make_async_copy(whole.at[:, lanes(place ^ (i + 1), share)], out, sem) for i, out in enumerate(outs)]
    for c in copies:
        c.start()
    return copies


def backward_kernel(start, sizes, terms, ready, direct, first, scale_in, rows_ref, cols_ref, *refs):
    parts, refs = refs[:terms * len(sizes)], refs[terms * len(sizes):]
    (tgt_hbm, fac, up, down, dep, also), refs = refs[:6], refs[6 if first else 8:]
    (back, send, err, dpre), outs, refs = refs[:4], refs[4:4 + direct], refs[5 + direct:]
    tgt, acc, table, count, sems = refs
    size, width = tgt.shape
    blocks, blk = up.shape[0], up.shape[1]
    mine = pl.ds(start, size)
    place = lax.axis_index("tensor")
    if not ready:
        copy = pltpu.make_async_copy(tgt_hbm.at[mine], tgt, sems.at[0])
        copy.start()
    column_table(cols_ref, table, count, blocks)
    acc[...] = jnp.zeros_like(acc)
    share = width // terms
    if ready:
        copies, offset = [], start
        for n, rows in enumerate(sizes):
            for i in range(terms):
                target = err.at[pl.ds(offset, rows), lanes(place ^ i, share)]
                copies.append(pltpu.make_async_copy(parts[n * terms + i], target, sems.at[0]))
                copies[-1].start()
            offset += rows
        for c in copies:
            c.wait()
    else:
        copy.wait()
        offset = 0
        for n, rows in enumerate(sizes):
            for b in range(width // blk):
                s = slice(b * blk, (b + 1) * blk)
                total = parts[n * terms][:, s].astype(f32)
                for i in range(1, terms):
                    total += parts[n * terms + i][:, s].astype(f32)
                err[pl.ds(start + offset, rows), s] = (total - tgt[pl.ds(offset, rows), s].astype(f32)).astype(bf16)
            offset += rows
    for h in range(blocks // per_column):
        dact = None
        for j in range(per_column):
            k = table[per_column * h + j]
            term = lax.dot_general(err[mine, lanes(rows_ref[k], blk)], down[k], NT, preferred_element_type=f32)
            dact = term if dact is None else dact + term
        s = slice(h * blk, (h + 1) * blk)
        dpre[mine, s] = (dact * fac[mine, s].astype(f32)).astype(bf16)
    for k in range(blocks):
        r = rows_ref[k]
        acc[r] += lax.dot_general(dpre[mine, lanes(cols_ref[k], blk)], up[k], NT, preferred_element_type=f32)
    for b in range(acc.shape[0]):
        back[:, b * blk:(b + 1) * blk] = (acc[b] * scale_in).astype(bf16)
    out = shares_of(back, outs, sems.at[1])
    if not direct and terms > 1:
        first_column = jnp.where(place == 0, share, 0)
        copy = pltpu.make_async_copy(back.at[:, pl.ds(pl.multiple_of(first_column, share), width - share)], send, sems.at[1])
        copy.start()
        out.append(copy)
    for c in out:
        c.wait()


def error_kernel(start, count, *refs):
    terms, (tgt_hbm, dep, also, o_ref, token, tgt, sem) = refs[:count], refs[count:]
    size, share = tgt.shape
    own = lanes(lax.axis_index("tensor"), share)
    copy = pltpu.make_async_copy(tgt_hbm.at[pl.ds(start, size), own], tgt, sem)
    copy.start()
    total = terms[0][:, own].astype(f32)
    for i in range(1, count):
        total += terms[i][...].astype(f32)
    copy.wait()
    o_ref[...] = (total - tgt[...].astype(f32)).astype(bf16)


def add_kernel(a_ref, b_ref, dep, also, o_ref, token):
    o_ref[...] = (a_ref[...].astype(f32) + b_ref[...].astype(f32)).astype(bf16)


def pass_on_kernel(hop, count, back, got, dep, also, o_ref, token):
    width = o_ref.shape[1]
    part = width // (count - hop)
    right = lax.axis_index("tensor") == hop - 1
    a = back[:, pl.ds(pl.multiple_of(jnp.where(right, hop * part, 0), part), width)]
    b = got[:, pl.ds(pl.multiple_of(jnp.where(right, part, 0), part), width)]
    o_ref[...] = (a.astype(f32) + b.astype(f32)).astype(bf16)


def finish_kernel(start, count, direct, *refs):
    terms, (old, dep, also, out_hbm, token, buf, sem) = refs[:count], refs[count:]
    size, part = buf.shape
    place = lax.axis_index("tensor")
    total = terms[0][:, lanes(place, part)].astype(f32)
    for j in range(1, count):
        if direct:
            total += terms[j][...].astype(f32)
        else:
            at = jnp.where(place == j, 0, (count - 1 - j) * part)
            total += terms[j][:, pl.ds(pl.multiple_of(at, part), part)].astype(f32)
    buf[...] = total.astype(bf16)
    copy = pltpu.make_async_copy(buf, out_hbm.at[pl.ds(start, size)], sem)
    copy.start()
    copy.wait()


def turn_kernel(act, tok_hbm, dep, also, act_t, tok_t, token, tok, sems):
    count, blk = act_t.shape[0], act_t.shape[1]
    columns = [slice(b * blk, (b + 1) * blk) for b in range(count)]
    copies = [pltpu.make_async_copy(tok_hbm.at[:, c], tok.at[:, c], sems.at[b]) for b, c in enumerate(columns)]
    for c in copies:
        c.start()
    for b, c in enumerate(columns):
        act_t[b] = act[:, c].T
    for b, c in enumerate(columns):
        copies[b].wait()
        tok_t[b] = tok[:, c].T


def grad_kernel(scale, by_hidden, rows_ref, cols_ref, left, right, own, peer_hbm, dep, also, out_hbm, token,
                peer, out, table, count, sems):
    blocks, blk = own.shape[0], own.shape[1]
    copies = [pltpu.make_async_copy(peer_hbm.at[k], peer.at[k], sems.at[0]) for k in range(blocks)]
    for c in copies:
        c.start()
    column_table(cols_ref, table, count, blocks)
    for c in copies:
        c.wait()
    done = []
    for h in range(blocks // per_column):
        for j in range(per_column):
            k = table[per_column * h + j]
            model = rows_ref[k]
            if by_hidden:
                grad = jnp.dot(left[h], right[:, lanes(model, blk)], preferred_element_type=f32)
            else:
                grad = jnp.dot(left[model], right[:, h * blk:(h + 1) * blk], preferred_element_type=f32)
            mixed = 0.5 * (own[k].astype(f32) + peer[k].astype(f32))
            out[k] = (mixed - (step_rate * scale) * grad).astype(bf16)
            done.append(pltpu.make_async_copy(out.at[k], out_hbm.at[k], sems.at[1]))
            done[-1].start()
    for c in done:
        c.wait()


def cut(total, shares, unit=16):
    edges = [0]
    for i in range(1, len(shares)):
        edges.append(round(total * sum(shares[:i]) / sum(shares) / unit) * unit)
    edges.append(total)
    return [(a, b - a) for a, b in zip(edges, edges[1:]) if b > a]


def on_device(shares, groups, direct_sum, direct_grad, tokens, targets, up_weight, down_weight, block_rows, block_columns):
    tok_count, width = tokens.shape
    up, down = up_weight[0], down_weight[0]
    blocks, blk = up.shape[0], up.shape[1]
    count = lax.axis_size("tensor")
    hops = count - 1
    hidden = blocks // per_column * blk
    scale_in = (width // 4) ** -0.5
    scale_out = (hidden * count // 4) ** -0.5
    level = (lax.axis_size("dp").bit_length() - 1) // 2
    part = width // count
    model_blocks = width // blk

    def hop(x, j):
        return lax.ppermute(x, "tensor", [(j - 1, j), (count - j, count - 1 - j)])

    def across(x, k):
        return lax.ppermute(x, "tensor", [(i, i ^ k) for i in range(count)])

    def partner(x):
        return lax.ppermute(x, "dp", [(i, i ^ (1 << level)) for i in range(lax.axis_size("dp"))])

    peer_up, peer_down = partner(up), partner(down)
    chunks = cut(tok_count, shares)
    C = len(chunks)
    like = lambda *s: jax.ShapeDtypeStruct(s, bf16)
    V = lambda *s: pltpu.VMEM(s, bf16)

    state = dict(act=None, fac=None, err=None, dpre=None, out=None, dep=block_rows)
    part_of, back_of, new = {}, {}, {}
    got = {}
    gotg = {}

    token = pltpu.HBM((16, 128), bf16)
    in_hbm = lambda x: pltpu.with_memory_space_constraint(x, pltpu.HBM)
    in_vmem = lambda x: pltpu.with_memory_space_constraint(x, pltpu.VMEM)
    weights = lambda: (in_vmem(state["up"]), in_vmem(state["down"]))

    spans = [(chunks[g[0]][0], sum(chunks[c][1] for c in g)) for g in groups]

    def after():
        return in_hbm(state["dep"]), in_hbm(state.pop("also", state["dep"]))

    def forward(c):
        start, size = chunks[c]
        first = c == 0
        direct = hops if c in direct_sum else 0
        scratch = [V(size, width), pltpu.VMEM((model_blocks, size, blk), f32),
                   pltpu.SMEM((blocks,), jnp.int32), pltpu.SMEM((blocks // per_column,), jnp.int32),
                   pltpu.SemaphoreType.DMA((6,))]
        held = (V(tok_count, hidden), V(tok_count, hidden))
        if first:
            scratch += [pltpu.SMEM((blocks,), jnp.int32), pltpu.SMEM((blocks,), jnp.int32)]
            a = [in_hbm(x) for x in (block_rows, block_columns, tokens, up, down, block_rows, block_rows)]
            specs, alias = [ANY] * 7, {}
            held += (V(*up.shape), V(*down.shape))
        else:
            a = [block_rows, block_columns, in_hbm(tokens), *weights(), *after(), in_vmem(state["act"]), in_vmem(state["fac"])]
            specs, alias = [SMEM, SMEM, ANY, ANYV, ANYV, ANY, ANY, ANYV, ANYV], {7: 1, 8: 2}
        p, act, fac, *outs = pl.pallas_call(
            functools.partial(forward_kernel, start, scale_in, scale_out, direct, first),
            out_shape=(V(size, width), *held) + (like(size, part),) * direct + (token,),
            in_specs=specs, out_specs=(ANYV,) * (1 + len(held) + direct) + (ANY,),
            input_output_aliases=alias, scratch_shapes=scratch,
            compiler_params=params(), name=f"forward_{c}", cost_estimate=cost(1, 1),
        )(*a)
        if first:
            state.update(up=outs.pop(0), down=outs.pop(0))
        *sends, done = outs
        state.update(act=act, fac=fac, dep=done)
        part_of[c] = p
        if direct:
            for i, x in enumerate(sends):
                got[c, i + 1] = across(x, i + 1)
        elif hops:
            got[c, 1] = hop(p, 1)

    def error(c):
        start, size = chunks[c]
        e, done = pl.pallas_call(
            functools.partial(error_kernel, start, count), out_shape=(like(size, part), token),
            in_specs=[ANYV] * count + [ANY] * 3, out_specs=(ANYV, ANY),
            scratch_shapes=[V(size, part), pltpu.SemaphoreType.DMA],
            compiler_params=params(), name=f"error_{c}", cost_estimate=cost(1, 1),
        )(part_of[c], *[got[c, i] for i in range(1, count)], in_hbm(targets), *after())
        state["dep"] = done
        got[c, 0] = e
        for i in range(1, count):
            got[c, i] = across(e, i)

    def add(c, j):
        start, size = chunks[c]
        s, done = pl.pallas_call(
            add_kernel, out_shape=(like(size, width), token),
            in_specs=[ANYV, ANYV, ANY, ANY], out_specs=(ANYV, ANY),
            compiler_params=params(), name=f"add_{c}_{j}", cost_estimate=cost(1, 1),
        )(part_of[c], got[c, j - 1], *after())
        state["dep"] = done
        got[c, j] = hop(s, j)

    def backward(c):
        start, size = spans[c]
        first = c == 0
        ready = groups[c][0] in direct_sum
        direct = hops if c in direct_grad else 0
        a = [block_rows, block_columns]
        for n in groups[c]:
            a += [got[n, 0] if ready else part_of[n]] + [got[n, j] for j in range(1, count)]
        a += [in_hbm(targets), in_vmem(state["fac"]), *weights(), *after()]
        specs = [SMEM, SMEM] + [ANYV] * (count * len(groups[c])) + [ANY] + [ANYV] * 3 + [ANY] * 2
        alias = {}
        if not first:
            alias = {len(a): 2, len(a) + 1: 3}
            a += [in_vmem(state["err"]), in_vmem(state["dpre"])]
            specs += [ANYV] * 2
        chain = like(size, width - part) if hops and not direct else like(16, 128)
        g, send, err, dpre, *sends, done = pl.pallas_call(
            functools.partial(backward_kernel, start, [chunks[n][1] for n in groups[c]], count, ready, direct, first, scale_in),
            out_shape=(V(size, width), chain, V(tok_count, width), V(tok_count, hidden)) + (like(size, part),) * direct + (token,),
            in_specs=specs, out_specs=(ANYV,) * (4 + direct) + (ANY,),
            input_output_aliases=alias,
            scratch_shapes=[V(size, width), pltpu.VMEM((model_blocks, size, blk), f32),
                            pltpu.SMEM((blocks,), jnp.int32), pltpu.SMEM((blocks // per_column,), jnp.int32),
                            pltpu.SemaphoreType.DMA((2,))],
            compiler_params=params(), name=f"backward_{c}", cost_estimate=cost(1, 1),
        )(*a)
        state.update(err=err, dpre=dpre, dep=done)
        back_of[c] = g
        if direct:
            for i, x in enumerate(sends):
                gotg[c, i + 1] = across(x, i + 1)
        elif hops:
            gotg[c, 1] = hop(send, 1)

    def pass_on(c, j):
        start, size = spans[c]
        wide = (count - j) * part
        s, done = pl.pallas_call(
            functools.partial(pass_on_kernel, j, count), out_shape=(like(size, wide), token),
            in_specs=[ANYV, ANYV, ANY, ANY], out_specs=(ANYV, ANY),
            compiler_params=params(), name=f"pass_on_{c}_{j}", cost_estimate=cost(1, 1),
        )(back_of[c], gotg[c, j - 1], *after())
        state["dep"] = done
        gotg[c, j] = hop(s, j)

    def finish(c):
        start, size = spans[c]
        first = state["out"] is None
        a = [back_of[c]] + [gotg[c, j] for j in range(1, count)] + [tokens if first else state["out"], *after()]
        o, done = pl.pallas_call(
            functools.partial(finish_kernel, start, count, c in direct_grad), out_shape=(like(tok_count, part), token),
            in_specs=[ANYV] * count + [ANY] * 3, out_specs=(ANY, ANY),
            input_output_aliases={} if first else {count: 0},
            scratch_shapes=[V(size, part), pltpu.SemaphoreType.DMA],
            compiler_params=params(), name=f"finish_{c}", cost_estimate=cost(size * width, 5 * size * width),
        )(*a)
        state.update(out=o, dep=done)

    def turn():
        turned = V(model_blocks, blk, tok_count)
        act_t, tok_t, done = pl.pallas_call(
            turn_kernel, out_shape=(turned, turned, token), in_specs=[ANYV] + [ANY] * 3, out_specs=(ANYV, ANYV, ANY),
            scratch_shapes=[V(tok_count, width), pltpu.SemaphoreType.DMA((model_blocks,))],
            compiler_params=params(), name="turn", cost_estimate=cost(1, 1),
        )(in_vmem(state["act"]), in_hbm(tokens), *after())
        state.update(act_t=act_t, tok_t=tok_t, dep=done)

    def grads(which):
        by_hidden = which == "down"
        own, scale = state[which], scale_out if by_hidden else scale_in
        if by_hidden:
            left, right, peer = state["act_t"], state["err"], peer_down
        else:
            left, right, peer = state["tok_t"], state["dpre"], peer_up
        o, done = pl.pallas_call(
            functools.partial(grad_kernel, scale, by_hidden), out_shape=(like(blocks, blk, blk), token),
            in_specs=[SMEM, SMEM] + [ANYV] * 3 + [ANY] * 3, out_specs=(ANY, ANY),
            scratch_shapes=[V(*own.shape), V(*own.shape),
                            pltpu.SMEM((blocks,), jnp.int32), pltpu.SMEM((blocks // per_column,), jnp.int32),
                            pltpu.SemaphoreType.DMA((2,))],
            compiler_params=params(), name=f"grad_{which}", cost_estimate=cost(1, 1),
        )(block_rows, block_columns, in_vmem(left), in_vmem(right), in_vmem(own), in_hbm(peer), *after())
        new[which] = o
        state["dep"] = done

    order = plan()
    for what, c, j in order:
        if what == "F":
            forward(c)
        elif what == "A":
            add(c, j)
        elif what == "S":
            error(c)
        elif what == "T":
            turn()
        elif what == "X":
            state["also"] = (peer_up, peer_down)[c]
        elif what == "B":
            backward(c)
        elif what == "P":
            pass_on(c, j)
        elif what == "E":
            finish(c)
        else:
            grads(what)
    return new["up"][None], new["down"][None], state["out"]


ORDER = (
    "F0", "F1", "F2", "A02", "F3", "A12", "A03", "T0", "A22", "X0", "A13", "B0", "A32", "A23", "B1", "P02", "A33",
    "B2", "X1", "P03", "P12", "B3", "P13", "P22", "D0", "P23", "E0", "E1", "P32", "U0", "P33", "E2", "E3",
)


def plan():
    named = {"D": "down", "U": "up"}
    out = []
    for word in ORDER:
        what = word[0]
        if what in named:
            out.append((named[what], 0, 0))
        else:
            out.append((what, int(word[1]), int(word[2]) if len(word) > 2 else 0))
    return out


SHARES = (192, 192, 192, 192)
GROUPS = ((0,), (1,), (2,), (3,))
DIRECT_SUM = ()
DIRECT_GRAD = ()


def solution(mesh):
    return jax.shard_map(
        functools.partial(on_device, SHARES, GROUPS, DIRECT_SUM, DIRECT_GRAD),
        mesh=mesh,
        in_specs=(P("dp", None), P("dp", None), P("dp", "tensor", None, None), P("dp", "tensor", None, None),
                  P("tensor"), P("tensor")),
        out_specs=(P("dp", "tensor", None, None), P("dp", "tensor", None, None), P("dp", "tensor")),
        check_vma=False,
    )
```

time: 361 us -> 159 us (0.44)
  waiting for transfers between devices: 201 us -> 49.1 us
  matrix products: 97.2 us -> 0 us
  starting transfers between devices: 2.17 us -> 54 us
  Pallas kernels: 0 us -> 50.7 us
  local copies, waits for them, and re-layouts: 36.2 us -> 2.67 us
  between operations: 14.6 us -> 1.39 us
  other arithmetic: 6.34 us -> 0 us
    psum x1 -> x0, waiting for transfers between devices: 121 us -> none  [on_device(): output_total = lax.psum(out_part, 'tensor').astype(jnp.float32)]
    dot_general x10 -> x0, matrix products: 97.2 us -> none  [the longest x1 20.9 us: on_device(): jnp.einsum('tnk,nd->tdk', second, row_select, precision=lax.Precision.HIG...]
    ppermute x2 -> x26, starting transfers between devices: 2.09 us -> 54 us  [the longest x24 51 us: hop(): return lax.ppermute(x, 'tensor', [(j - 1, j), (count - j, count - 1 - j)])]
    pallas_call x0 -> x31, Pallas kernels: none -> 50.7 us  [the longest x4 17.7 us: backward(): pl.pallas_call(functools.partial(backward_kernel, start, [chunks[n][1] fo...]
    ppermute x2 -> x26, waiting for transfers between devices: 80.6 us -> 49.1 us  [the longest x24 49.1 us: hop(): return lax.ppermute(x, 'tensor', [(j - 1, j), (count - j, count - 1 - j)])]
    gather x4 -> x0, local copies, waits for them, and re-layouts: 14.3 us -> none  [the longest x1 3.61 us: on_device(): active_blocks = jnp.take(active, block_columns, axis=1)]
    unnamed x11 -> x14, local copies, waits for them, and re-layouts: 10.6 us -> 2.67 us
    reshape x2 -> x0, local copies, waits for them, and re-layouts: 6.33 us -> none  [the longest x1 3.17 us: on_device(): error_full.reshape(tok_count, model_blocks, block_size)]
  transfers between devices with their start and end apart: 4 -> 26, of which waited for: 3 -> 11; matrix products, arithmetic and copies ran while one was open for 6% -> 0% of each run, Pallas kernels for 0% -> 29%
where the time goes in v1:
time: 159 us; the launch traced here: 158 us
  starting transfers between devices  54 us (34%)
  Pallas kernels  50.7 us (32%)
  waiting for transfers between devices  49.1 us (31%)
  local copies, waits for them, and re-layouts  2.67 us (2%)
    ppermute x24, starting transfers between devices, hop(): return lax.ppermute(x, 'tensor', [(j - 1, j), (count - j, count - 1 - j)])  51 us
    ppermute x24, waiting for transfers between devices, hop(): return lax.ppermute(x, 'tensor', [(j - 1, j), (count - j, count - 1 - j)])  49.1 us
    pallas_call x4, Pallas kernels, backward(): pl.pallas_call(functools.partial(backward_kernel, start, [chunks[n][1] fo...  17.7 us
    pallas_call x4, Pallas kernels, forward(): pl.pallas_call(functools.partial(forward_kernel, start, scale_in, scale_o...  15 us
    pallas_call x2, Pallas kernels, grads(): pl.pallas_call(functools.partial(grad_kernel, scale, by_hidden), out_shap...  10.3 us
    pallas_call x4, Pallas kernels, finish(): pl.pallas_call(functools.partial(finish_kernel, start, count, c in direct...  3.19 us
  transfers between devices with their start and end apart: 26, of which 11 were waited for; matrix products, arithmetic and copies ran while one was open for 0% of the time, Pallas kernels for 29%

profile of v1, /device:TPU:0, one launch (start us, length us, event | category | flops | bytes accessed | tf_op | source)
XLA Modules:
  0.0 157.8 jit_solution(15395806088360836213)
XLA Ops:
  0.7 3.9 %forward_0.1 = (bf16[192,2048]{1,0:T(8,128)(2,1)S(1)}, bf16[768,2048]{1,0:T(8,128)(2,1)S(1)}, bf16[768,2048]{1,0:T(8,128)(2,1)S(1)}, bf16[16,256,256]{2,1,0:T(8,...) custom-call(s32[16]{0:T(128)} %rows_ref.19, s32[16]{0:T(128)} %cols_ref.19, ...), custom_call_target="tpu_custom_call" | custom-call | flops 1 | bytes 1 | tf_op jit(solution)/shard_map/forward_0/pallas_call | solution.py:314
  4.6 5.0 %collective-permute-start = (bf16[192,2048]{1,0:T(8,128)(2,1)S(1)}, bf16[192,2048]{1,0:T(8,128)(2,1)S(1)}, u32[]{:S(2)}, u32[]{:S(2)}) collective-permute-start(bf16[192,2048]{1,0:T(8,128)(2,1)S(1)} %get-tuple-element.89.a_ref.refs_0_), channel_id=1, source_target_pairs={{0,1},{3,2},{4,5},{7,6},{8,9},{11,10},{12,13},{15,14},{16,17},{19,... | collective-permute-start | bytes 2359304 | tf_op jit(solution)/shard_map/ppermute | solution.py:269
  9.6 1.5 collective-permute-start.7
  11.1 3.7 %forward_1.1 = (bf16[192,2048]{1,0:T(8,128)(2,1)S(1)}, bf16[768,2048]{1,0:T(8,128)(2,1)S(1)}, bf16[768,2048]{1,0:T(8,128)(2,1)S(1)}, bf16[16,128]{1,0:T(8,128)(2,1)}) custom-call(s32[16]{0:T(128)S(1)} %copy-done.1, s32[16]{0:T(128)S(1)} %copy-done.2, bf16[768,2048]{1,0:T(8,128)(2,1)} %refs_4_.9, ...), custom_call_target="tpu_custom_call", output_to_operand_aliasing={{1}: (7, {}), {2}: (8, {})} | custom-call | flops 1 | bytes 1 | tf_op jit(solution)/shard_map/forward_1/pallas_call | solution.py:314
  14.8 1.3 collective-permute-start.2
  16.2 3.7 %forward_2.1 = (bf16[192,2048]{1,0:T(8,128)(2,1)S(1)}, bf16[768,2048]{1,0:T(8,128)(2,1)S(1)}, bf16[768,2048]{1,0:T(8,128)(2,1)S(1)}, bf16[16,128]{1,0:T(8,128)(2,1)}) custom-call(s32[16]{0:T(128)S(1)} %copy-done.1, s32[16]{0:T(128)S(1)} %copy-done.2, bf16[768,2048]{1,0:T(8,128)(2,1)} %refs_4_.9, ...), custom_call_target="tpu_custom_call", output_to_operand_aliasing={{1}: (7, {}), {2}: (8, {})} | custom-call | flops 1 | bytes 1 | tf_op jit(solution)/shard_map/forward_2/pallas_call | solution.py:314
  19.9 7.6 %collective-permute-done.b_ref.refs_1_ = bf16[192,2048]{1,0:T(8,128)(2,1)S(1)} collective-permute-done((bf16[192,2048]{1,0:T(8,128)(2,1)S(1)}, bf16[192,2048]{1,0:T(8,128)(2,1)S(1)}, u32[]{:S(2)}, u32[]{:S(2)}) %collective-permute-start) | collective-permute-done | bytes 786464 | tf_op jit(solution)/shard_map/ppermute | solution.py:269
  27.5 0.2 add_0_2.1
  27.6 0.7 collective-permute-start.1
  28.4 7.2 %collective-permute-start.6 = (bf16[192,2048]{1,0:T(8,128)(2,1)S(1)}, bf16[192,2048]{1,0:T(8,128)(2,1)S(1)}, u32[]{:S(2)}, u32[]{:S(2)}) collective-permute-start(bf16[192,2048]{1,0:T(8,128)(2,1)S(1)} %get-tuple-element.111.a_ref.refs_0_), channel_id=1, source_target_pairs={{0,1},{3,2},{4,5},{7,6},{8,9},{11,10},{12,13},{15,14},{16,17},{19,... | collective-permute-start | bytes 2359304 | tf_op jit(solution)/shard_map/ppermute | solution.py:269
  35.5 3.7 %forward_3.1 = (bf16[192,2048]{1,0:T(8,128)(2,1)S(1)}, bf16[768,2048]{1,0:T(8,128)(2,1)S(1)}, bf16[768,2048]{1,0:T(8,128)(2,1)S(1)}, bf16[16,128]{1,0:T(8,128)(2,1)}) custom-call(s32[16]{0:T(128)S(1)} %copy-done.1, s32[16]{0:T(128)S(1)} %copy-done.2, bf16[768,2048]{1,0:T(8,128)(2,1)} %refs_4_.9, ...), custom_call_target="tpu_custom_call", output_to_operand_aliasing={{1}: (7, {}), {2}: (8, {})} | custom-call | flops 1 | bytes 1 | tf_op jit(solution)/shard_map/forward_3/pallas_call | solution.py:314
  39.3 5.0 %collective-permute-done.2.b_ref.refs_1_ = bf16[192,2048]{1,0:T(8,128)(2,1)S(1)} collective-permute-done((bf16[192,2048]{1,0:T(8,128)(2,1)S(1)}, bf16[192,2048]{1,0:T(8,128)(2,1)S(1)}, u32[]{:S(2)}, u32[]{:S(2)}) %collective-permute-start.2) | collective-permute-done | bytes 786464 | tf_op jit(solution)/shard_map/ppermute | solution.py:269
  44.3 0.2 add_1_2.1
  44.5 0.7 collective-permute-start.5
  45.2 0.2 add_0_3.1
  45.4 1.3 collective-permute-start.4
  46.7 7.2 %collective-permute-start.3 = (bf16[192,2048]{1,0:T(8,128)(2,1)S(1)}, bf16[192,2048]{1,0:T(8,128)(2,1)S(1)}, u32[]{:S(2)}, u32[]{:S(2)}) collective-permute-start(bf16[192,2048]{1,0:T(8,128)(2,1)S(1)} %get-tuple-element.107.a_ref.refs_0_), channel_id=1, source_target_pairs={{0,1},{3,2},{4,5},{7,6},{8,9},{11,10},{12,13},{15,14},{16,17},{19,... | collective-permute-start | bytes 2359304 | tf_op jit(solution)/shard_map/ppermute | solution.py:269
  53.9 7.2 %collective-permute-done.6.b_ref.refs_1_ = bf16[192,2048]{1,0:T(8,128)(2,1)S(1)} collective-permute-done((bf16[192,2048]{1,0:T(8,128)(2,1)S(1)}, bf16[192,2048]{1,0:T(8,128)(2,1)S(1)}, u32[]{:S(2)}, u32[]{:S(2)}) %collective-permute-start.6) | collective-permute-done | bytes 786464 | tf_op jit(solution)/shard_map/ppermute | solution.py:269
  61.2 1.5 collective-permute-start.16
  62.6 2.4 %turn.1 = (bf16[8,256,768]{2,1,0:T(8,128)(2,1)S(1)}, bf16[8,256,768]{2,1,0:T(8,128)(2,1)S(1)}, bf16[16,128]{1,0:T(8,128)(2,1)}) custom-call(bf16[768,2048]{1,0:T(8,128)(2,1)S(1)} %get-tuple-element.100.act, bf16[768,2048]{1,0:T(8,128)(2,1)} %refs_4_.9, bf16[16,128]{1,0:T(8,128)(2,1)} %get-tuple-element.105.dep.also, bf16[16,128]{1,0:T(8,128)(2,1)} %get-tuple-element.105.dep.also), custom_call_target="tpu_custom_call" | custom-call | flops 1 | bytes 1 | tf_op jit(solution)/shard_map/turn/pallas_call | solution.py:415
  65.0 0.2 add_2_2.1
  65.2 0.7 collective-permute-start.11
  66.0 1.3 copy-done.4
  67.3 0.2 add_1_3.1
  67.5 1.5 collective-permute-start.10
  69.0 4.4 %backward_0.1 = (bf16[192,2048]{1,0:T(8,128)(2,1)S(1)}, bf16[192,1536]{1,0:T(8,128)(2,1)S(1)}, bf16[768,2048]{1,0:T(8,128)(2,1)S(1)}, bf16[768,2048]{1,0:T(8,128)(2,1)S(1)}, bf16[16,128]{1,0:T(8,128)(2,1)}) custom-call(s32[16]{0:T(128)S(1)} %copy-done.1, s32[16]{0:T(128)S(1)} %copy-done.2, bf16[192,2048]{1,0:T(8,128)(2,1)S(1)} %get-tuple-element.89.a_ref.refs_0_, ...), custom_call_target="tpu_custom_call" | custom-call | flops 1 | bytes 1 | tf_op jit(solution)/shard_map/backward_0/pallas_call | solution.py:371
  73.4 3.4 %collective-permute-done.3.b_ref.refs_1_ = bf16[192,2048]{1,0:T(8,128)(2,1)S(1)} collective-permute-done((bf16[192,2048]{1,0:T(8,128)(2,1)S(1)}, bf16[192,2048]{1,0:T(8,128)(2,1)S(1)}, u32[]{:S(2)}, u32[]{:S(2)}) %collective-permute-start.3) | collective-permute-done | bytes 786464 | tf_op jit(solution)/shard_map/ppermute | solution.py:269
  76.8 0.2 add_3_2.1
  77.0 0.7 collective-permute-start.8
  77.7 7.2 %collective-permute-start.9 = (bf16[192,1536]{1,0:T(8,128)(2,1)S(1)}, bf16[192,1536]{1,0:T(8,128)(2,1)S(1)}, u32[]{:S(2)}, u32[]{:S(2)}) collective-permute-start(bf16[192,1536]{1,0:T(8,128)(2,1)S(1)} %get-tuple-element.118), channel_id=1, source_target_pairs={{0,1},{3,2},{4,5},{7,6},{8,9},{11,10},{12,13},{15,14},{16,17},{19,... | collective-permute-start | bytes 1769480 | tf_op jit(solution)/shard_map/ppermute | solution.py:269
  85.0 0.2 add_2_3.1
  85.1 1.3 collective-permute-start.15
  86.4 3.4 %collective-permute-done.10.refs_3_ = bf16[192,2048]{1,0:T(8,128)(2,1)S(1)} collective-permute-done((bf16[192,2048]{1,0:T(8,128)(2,1)S(1)}, bf16[192,2048]{1,0:T(8,128)(2,1)S(1)}, u32[]{:S(2)}, u32[]{:S(2)}) %collective-permute-start.10) | collective-permute-done | bytes 786464 | tf_op jit(solution)/shard_map/ppermute | solution.py:269
  89.8 4.4 %backward_1.1 = (bf16[192,2048]{1,0:T(8,128)(2,1)S(1)}, bf16[192,1536]{1,0:T(8,128)(2,1)S(1)}, bf16[768,2048]{1,0:T(8,128)(2,1)S(1)}, bf16[768,2048]{1,0:T(8,128)(2,1)S(1)}, bf16[16,128]{1,0:T(8,128)(2,1)}) custom-call(s32[16]{0:T(128)S(1)} %copy-done.1, s32[16]{0:T(128)S(1)} %copy-done.2, ...), custom_call_target="tpu_custom_call", output_to_operand_aliasing={{2}: (12, {}), {3}: (13, {})} | custom-call | flops 1 | bytes 1 | tf_op jit(solution)/shard_map/backward_1/pallas_call | solution.py:371
  94.3 3.7 %collective-permute-start.13 = (bf16[192,1536]{1,0:T(8,128)(2,1)S(1)}, bf16[192,1536]{1,0:T(8,128)(2,1)S(1)}, u32[]{:S(2)}, u32[]{:S(2)}) collective-permute-start(bf16[192,1536]{1,0:T(8,128)(2,1)S(1)} %get-tuple-element.129), channel_id=1, source_target_pairs={{0,1},{3,2},{4,5},{7,6},{8,9},{11,10},{12,13},{15,14},{16,17},{19,... | collective-permute-start | bytes 1769480 | tf_op jit(solution)/shard_map/ppermute | solution.py:269
  98.0 0.7 collective-permute-done.9.got.refs_1_
  98.8 0.2 add_3_3.1
  99.0 1.3 collective-permute-start.12
  100.3 0.7 collective-permute-start.14
  101.0 8.3 %collective-permute-done.15.refs_3_ = bf16[192,2048]{1,0:T(8,128)(2,1)S(1)} collective-permute-done((bf16[192,2048]{1,0:T(8,128)(2,1)S(1)}, bf16[192,2048]{1,0:T(8,128)(2,1)S(1)}, u32[]{:S(2)}, u32[]{:S(2)}) %collective-permute-start.15) | collective-permute-done | bytes 786464 | tf_op jit(solution)/shard_map/ppermute | solution.py:269
  109.2 4.4 %backward_2.1 = (bf16[192,2048]{1,0:T(8,128)(2,1)S(1)}, bf16[192,1536]{1,0:T(8,128)(2,1)S(1)}, bf16[768,2048]{1,0:T(8,128)(2,1)S(1)}, bf16[768,2048]{1,0:T(8,128)(2,1)S(1)}, bf16[16,128]{1,0:T(8,128)(2,1)}) custom-call(s32[16]{0:T(128)S(1)} %copy-done.1, s32[16]{0:T(128)S(1)} %copy-done.2, ...), custom_call_target="tpu_custom_call", output_to_operand_aliasing={{2}: (12, {}), {3}: (13, {})} | custom-call | flops 1 | bytes 1 | tf_op jit(solution)/shard_map/backward_2/pallas_call | solution.py:371
  113.6 1.5 collective-permute-start.21
  115.2 1.3 copy-done.3
  116.5 0.1 pass_on_1_2.1
  116.6 0.7 collective-permute-start.18
  117.3 5.3 %collective-permute-done.12.refs_3_ = bf16[192,2048]{1,0:T(8,128)(2,1)S(1)} collective-permute-done((bf16[192,2048]{1,0:T(8,128)(2,1)S(1)}, bf16[192,2048]{1,0:T(8,128)(2,1)S(1)}, u32[]{:S(2)}, u32[]{:S(2)}) %collective-permute-start.12) | collective-permute-done | bytes 786464 | tf_op jit(solution)/shard_map/ppermute | solution.py:269
  122.7 4.4 %backward_3.1 = (bf16[192,2048]{1,0:T(8,128)(2,1)S(1)}, bf16[192,1536]{1,0:T(8,128)(2,1)S(1)}, bf16[768,2048]{1,0:T(8,128)(2,1)S(1)}, bf16[768,2048]{1,0:T(8,128)(2,1)S(1)}, bf16[16,128]{1,0:T(8,128)(2,1)}) custom-call(s32[16]{0:T(128)S(1)} %copy-done.1, s32[16]{0:T(128)S(1)} %copy-done.2, ...), custom_call_target="tpu_custom_call", output_to_operand_aliasing={{2}: (12, {}), {3}: (13, {})} | custom-call | flops 1 | bytes 1 | tf_op jit(solution)/shard_map/backward_3/pallas_call | solution.py:371
  127.1 1.5 collective-permute-start.17
  128.7 0.1 pass_on_2_2.1
  128.8 0.7 collective-permute-start.22
  129.5 1.3 collective-permute-start.20
  130.8 1.5 collective-permute-start.19
  132.3 5.3 %grad_down.1 = (bf16[16,256,256]{2,1,0:T(8,128)(2,1)}, bf16[16,128]{1,0:T(8,128)(2,1)}) custom-call(s32[16]{0:T(128)S(1)} %copy-done.1, s32[16]{0:T(128)S(1)} %copy-done.2, bf16[8,256,768]{2,1,0:T(8,128)(2,1)S(1)} %get-tuple-element.151.left, bf16[768,2048]{1,0:T(8,128)(2,1)S(1)} %get-tuple-element.152.right, ...), custom_call_target="tpu_custom_call" | custom-call | flops 1 | bytes 1 | tf_op jit(solution)/shard_map/grad_down/pallas_call | solution.py:429
  137.8 0.8 finish_0.1
  138.6 0.6 collective-permute-done.19.refs_3_
  139.2 0.8 finish_1.1
  140.1 0.7 collective-permute-start.23
  140.8 1.3 collective-permute-start.25
  142.1 5.0 %grad_up.1 = (bf16[16,256,256]{2,1,0:T(8,128)(2,1)}, bf16[16,128]{1,0:T(8,128)(2,1)}) custom-call(s32[16]{0:T(128)S(1)} %copy-done.1, s32[16]{0:T(128)S(1)} %copy-done.2, bf16[8,256,768]{2,1,0:T(8,128)(2,1)S(1)} %get-tuple-element.106.left, bf16[768,2048]{1,0:T(8,128)(2,1)S(1)} %get-tuple-element.140.right, ...), custom_call_target="tpu_custom_call" | custom-call | flops 1 | bytes 1 | tf_op jit(solution)/shard_map/grad_up/pallas_call | solution.py:429
  147.2 1.3 collective-permute-start.24
  148.5 1.0 collective-permute-done.25.refs_3_
  149.5 0.8 finish_2.1
  150.3 6.6 %collective-permute-done.24.refs_3_ = bf16[192,512]{1,0:T(8,128)(2,1)S(1)} collective-permute-done((bf16[192,512]{1,0:T(8,128)(2,1)S(1)}, bf16[192,512]{1,0:T(8,128)(2,1)S(1)}, u32[]{:S(2)}, u32[]{:S(2)}) %collective-permute-start.24) | collective-permute-done | bytes 196640 | tf_op jit(solution)/shard_map/ppermute | solution.py:269
  156.8 0.8 finish_3.1
  (33 shorter events, 0.5 us)
Async XLA Ops:
  0.6 8.9 %copy-start.5 = (bf16[1,16,256,256]{3,2,1,0:T(8,128)(2,1)S(1)}, bf16[1,16,256,256]{3,2,1,0:T(8,128)(2,1)}, u32[]{:S(2)}) copy-start(bf16[1,16,256,256]{3,2,1,0:T(8,128)(2,1)} %param.8) | copy-start | bytes 6291460
  0.6 10.5 %copy-start.1 = (s32[16]{0:T(128)S(1)}, s32[16]{0:T(128)}, u32[]{:S(2)}) copy-start(s32[16]{0:T(128)} %rows_ref.19) | copy-start | bytes 196
  0.7 10.5 %copy-start.2 = (s32[16]{0:T(128)S(1)}, s32[16]{0:T(128)}, u32[]{:S(2)}) copy-start(s32[16]{0:T(128)} %cols_ref.19) | copy-start | bytes 196
  4.6 22.9 %collective-permute-start = (bf16[192,2048]{1,0:T(8,128)(2,1)S(1)}, bf16[192,2048]{1,0:T(8,128)(2,1)S(1)}, u32[]{:S(2)}, u32[]{:S(2)}) collective-permute-start(bf16[192,2048]{1,0:T(8,128)(2,1)S(1)} %get-tuple-element.89.a_ref.refs_0_), channel_id=1, source_target_pairs={{0,1},{3,2},{4,5},{7,6},{8,9},{11,10},{12,13},{15,14},{16,17},{19,... | collective-permute-start | bytes 2359304 | tf_op jit(solution)/shard_map/ppermute | solution.py:269
  9.6 56.4 %collective-permute-start.7 = (bf16[16,256,256]{2,1,0:T(8,128)(2,1)S(1)}, bf16[16,256,256]{2,1,0:T(8,128)(2,1)S(1)}, u32[]{:S(2)}, u32[]{:S(2)}) collective-permute-start(bf16[16,256,256]{2,1,0:T(8,128)(2,1)S(1)} %bitcast.5), channel_id=1, source_target_pairs={{0,8},{4,12},{8,0},{12,4},{16,24},{20,28},{24,16},{28,20},{1,9},{5... | collective-permute-start | bytes 6291464 | tf_op jit(solution)/shard_map/ppermute | solution.py:275
  14.8 29.5 %collective-permute-start.2 = (bf16[192,2048]{1,0:T(8,128)(2,1)S(1)}, bf16[192,2048]{1,0:T(8,128)(2,1)S(1)}, u32[]{:S(2)}, u32[]{:S(2)}) collective-permute-start(bf16[192,2048]{1,0:T(8,128)(2,1)S(1)} %get-tuple-element.102.a_ref.refs_0_), channel_id=1, source_target_pairs={{0,1},{3,2},{4,5},{7,6},{8,9},{11,10},{12,13},{15,14},{16,17},{19,... | collective-permute-start | bytes 2359304 | tf_op jit(solution)/shard_map/ppermute | solution.py:269
  27.6 17.6 %collective-permute-start.1 = (bf16[192,2048]{1,0:T(8,128)(2,1)S(1)}, bf16[192,2048]{1,0:T(8,128)(2,1)S(1)}, u32[]{:S(2)}, u32[]{:S(2)}) collective-permute-start(bf16[192,2048]{1,0:T(8,128)(2,1)S(1)} %get-tuple-element.101), channel_id=1, source_target_pairs={{1,2},{2,1},{5,6},{6,5},{9,10},{10,9},{13,14},{14,13},{17,18},{18,... | collective-permute-start | bytes 2359304 | tf_op jit(solution)/shard_map/ppermute | solution.py:269
  28.4 32.8 %collective-permute-start.6 = (bf16[192,2048]{1,0:T(8,128)(2,1)S(1)}, bf16[192,2048]{1,0:T(8,128)(2,1)S(1)}, u32[]{:S(2)}, u32[]{:S(2)}) collective-permute-start(bf16[192,2048]{1,0:T(8,128)(2,1)S(1)} %get-tuple-element.111.a_ref.refs_0_), channel_id=1, source_target_pairs={{0,1},{3,2},{4,5},{7,6},{8,9},{11,10},{12,13},{15,14},{16,17},{19,... | collective-permute-start | bytes 2359304 | tf_op jit(solution)/shard_map/ppermute | solution.py:269
  39.3 21.9 %copy-start.6 = (bf16[1,16,256,256]{3,2,1,0:T(8,128)(2,1)S(1)}, bf16[1,16,256,256]{3,2,1,0:T(8,128)(2,1)}, u32[]{:S(2)}) copy-start(bf16[1,16,256,256]{3,2,1,0:T(8,128)(2,1)} %param.9) | copy-start | bytes 6291460
  44.5 20.7 %collective-permute-start.5 = (bf16[192,2048]{1,0:T(8,128)(2,1)S(1)}, bf16[192,2048]{1,0:T(8,128)(2,1)S(1)}, u32[]{:S(2)}, u32[]{:S(2)}) collective-permute-start(bf16[192,2048]{1,0:T(8,128)(2,1)S(1)} %get-tuple-element.110), channel_id=1, source_target_pairs={{1,2},{2,1},{5,6},{6,5},{9,10},{10,9},{13,14},{14,13},{17,18},{18,... | collective-permute-start | bytes 2359304 | tf_op jit(solution)/shard_map/ppermute | solution.py:269
  45.4 23.6 %collective-permute-start.4 = (bf16[192,2048]{1,0:T(8,128)(2,1)S(1)}, bf16[192,2048]{1,0:T(8,128)(2,1)S(1)}, u32[]{:S(2)}, u32[]{:S(2)}) collective-permute-start(bf16[192,2048]{1,0:T(8,128)(2,1)S(1)} %get-tuple-element.108), channel_id=1, source_target_pairs={{2,3},{1,0},{6,7},{5,4},{10,11},{9,8},{14,15},{13,12},{18,19},{17,... | collective-permute-start | bytes 2359304 | tf_op jit(solution)/shard_map/ppermute | solution.py:269
  46.7 30.1 %collective-permute-start.3 = (bf16[192,2048]{1,0:T(8,128)(2,1)S(1)}, bf16[192,2048]{1,0:T(8,128)(2,1)S(1)}, u32[]{:S(2)}, u32[]{:S(2)}) collective-permute-start(bf16[192,2048]{1,0:T(8,128)(2,1)S(1)} %get-tuple-element.107.a_ref.refs_0_), channel_id=1, source_target_pairs={{0,1},{3,2},{4,5},{7,6},{8,9},{11,10},{12,13},{15,14},{16,17},{19,... | collective-permute-start | bytes 2359304 | tf_op jit(solution)/shard_map/ppermute | solution.py:269
  61.2 54.0 %collective-permute-start.16 = (bf16[16,256,256]{2,1,0:T(8,128)(2,1)S(1)}, bf16[16,256,256]{2,1,0:T(8,128)(2,1)S(1)}, u32[]{:S(2)}, u32[]{:S(2)}) collective-permute-start(bf16[16,256,256]{2,1,0:T(8,128)(2,1)S(1)} %bitcast.7), channel_id=1, source_target_pairs={{0,8},{4,12},{8,0},{12,4},{16,24},{20,28},{24,16},{28,20},{1,9},{5... | collective-permute-start | bytes 6291464 | tf_op jit(solution)/shard_map/ppermute | solution.py:275
  65.2 19.7 %collective-permute-start.11 = (bf16[192,2048]{1,0:T(8,128)(2,1)S(1)}, bf16[192,2048]{1,0:T(8,128)(2,1)S(1)}, u32[]{:S(2)}, u32[]{:S(2)}) collective-permute-start(bf16[192,2048]{1,0:T(8,128)(2,1)S(1)} %get-tuple-element.120), channel_id=1, source_target_pairs={{1,2},{2,1},{5,6},{6,5},{9,10},{10,9},{13,14},{14,13},{17,18},{18,... | collective-permute-start | bytes 2359304 | tf_op jit(solution)/shard_map/ppermute | solution.py:269
  65.9 1.4 copy-start.4
  67.5 22.4 %collective-permute-start.10 = (bf16[192,2048]{1,0:T(8,128)(2,1)S(1)}, bf16[192,2048]{1,0:T(8,128)(2,1)S(1)}, u32[]{:S(2)}, u32[]{:S(2)}) collective-permute-start(bf16[192,2048]{1,0:T(8,128)(2,1)S(1)} %get-tuple-element.119), channel_id=1, source_target_pairs={{2,3},{1,0},{6,7},{5,4},{10,11},{9,8},{14,15},{13,12},{18,19},{17,... | collective-permute-start | bytes 2359304 | tf_op jit(solution)/shard_map/ppermute | solution.py:269
  77.0 21.7 %collective-permute-start.8 = (bf16[192,2048]{1,0:T(8,128)(2,1)S(1)}, bf16[192,2048]{1,0:T(8,128)(2,1)S(1)}, u32[]{:S(2)}, u32[]{:S(2)}) collective-permute-start(bf16[192,2048]{1,0:T(8,128)(2,1)S(1)} %get-tuple-element.116), channel_id=1, source_target_pairs={{1,2},{2,1},{5,6},{6,5},{9,10},{10,9},{13,14},{14,13},{17,18},{18,... | collective-permute-start | bytes 2359304 | tf_op jit(solution)/shard_map/ppermute | solution.py:269
  77.7 20.9 %collective-permute-start.9 = (bf16[192,1536]{1,0:T(8,128)(2,1)S(1)}, bf16[192,1536]{1,0:T(8,128)(2,1)S(1)}, u32[]{:S(2)}, u32[]{:S(2)}) collective-permute-start(bf16[192,1536]{1,0:T(8,128)(2,1)S(1)} %get-tuple-element.118), channel_id=1, source_target_pairs={{0,1},{3,2},{4,5},{7,6},{8,9},{11,10},{12,13},{15,14},{16,17},{19,... | collective-permute-start | bytes 1769480 | tf_op jit(solution)/shard_map/ppermute | solution.py:269
  85.1 24.1 %collective-permute-start.15 = (bf16[192,2048]{1,0:T(8,128)(2,1)S(1)}, bf16[192,2048]{1,0:T(8,128)(2,1)S(1)}, u32[]{:S(2)}, u32[]{:S(2)}) collective-permute-start(bf16[192,2048]{1,0:T(8,128)(2,1)S(1)} %get-tuple-element.131), channel_id=1, source_target_pairs={{2,3},{1,0},{6,7},{5,4},{10,11},{9,8},{14,15},{13,12},{18,19},{17,... | collective-permute-start | bytes 2359304 | tf_op jit(solution)/shard_map/ppermute | solution.py:269
  94.3 22.2 %collective-permute-start.13 = (bf16[192,1536]{1,0:T(8,128)(2,1)S(1)}, bf16[192,1536]{1,0:T(8,128)(2,1)S(1)}, u32[]{:S(2)}, u32[]{:S(2)}) collective-permute-start(bf16[192,1536]{1,0:T(8,128)(2,1)S(1)} %get-tuple-element.129), channel_id=1, source_target_pairs={{0,1},{3,2},{4,5},{7,6},{8,9},{11,10},{12,13},{15,14},{16,17},{19,... | collective-permute-start | bytes 1769480 | tf_op jit(solution)/shard_map/ppermute | solution.py:269
  99.0 23.7 %collective-permute-start.12 = (bf16[192,2048]{1,0:T(8,128)(2,1)S(1)}, bf16[192,2048]{1,0:T(8,128)(2,1)S(1)}, u32[]{:S(2)}, u32[]{:S(2)}) collective-permute-start(bf16[192,2048]{1,0:T(8,128)(2,1)S(1)} %get-tuple-element.127), channel_id=1, source_target_pairs={{2,3},{1,0},{6,7},{5,4},{10,11},{9,8},{14,15},{13,12},{18,19},{17,... | collective-permute-start | bytes 2359304 | tf_op jit(solution)/shard_map/ppermute | solution.py:269
  100.3 14.9 %collective-permute-start.14 = (bf16[192,1024]{1,0:T(8,128)(2,1)S(1)}, bf16[192,1024]{1,0:T(8,128)(2,1)S(1)}, u32[]{:S(2)}, u32[]{:S(2)}) collective-permute-start(bf16[192,1024]{1,0:T(8,128)(2,1)S(1)} %get-tuple-element.130), channel_id=1, source_target_pairs={{1,2},{2,1},{5,6},{6,5},{9,10},{10,9},{13,14},{14,13},{17,18},{18,... | collective-permute-start | bytes 1179656 | tf_op jit(solution)/shard_map/ppermute | solution.py:269
  113.6 15.0 %collective-permute-start.21 = (bf16[192,1536]{1,0:T(8,128)(2,1)S(1)}, bf16[192,1536]{1,0:T(8,128)(2,1)S(1)}, u32[]{:S(2)}, u32[]{:S(2)}) collective-permute-start(bf16[192,1536]{1,0:T(8,128)(2,1)S(1)} %get-tuple-element.148), channel_id=1, source_target_pairs={{0,1},{3,2},{4,5},{7,6},{8,9},{11,10},{12,13},{15,14},{16,17},{19,... | collective-permute-start | bytes 1769480 | tf_op jit(solution)/shard_map/ppermute | solution.py:269
  115.1 1.3 copy-start.3
  116.6 12.0 %collective-permute-start.18 = (bf16[192,1024]{1,0:T(8,128)(2,1)S(1)}, bf16[192,1024]{1,0:T(8,128)(2,1)S(1)}, u32[]{:S(2)}, u32[]{:S(2)}) collective-permute-start(bf16[192,1024]{1,0:T(8,128)(2,1)S(1)} %get-tuple-element.143), channel_id=1, source_target_pairs={{1,2},{2,1},{5,6},{6,5},{9,10},{10,9},{13,14},{14,13},{17,18},{18,... | collective-permute-start | bytes 1179656 | tf_op jit(solution)/shard_map/ppermute | solution.py:269
  127.1 12.9 %collective-permute-start.17 = (bf16[192,1536]{1,0:T(8,128)(2,1)S(1)}, bf16[192,1536]{1,0:T(8,128)(2,1)S(1)}, u32[]{:S(2)}, u32[]{:S(2)}) collective-permute-start(bf16[192,1536]{1,0:T(8,128)(2,1)S(1)} %get-tuple-element.142), channel_id=1, source_target_pairs={{0,1},{3,2},{4,5},{7,6},{8,9},{11,10},{12,13},{15,14},{16,17},{19,... | collective-permute-start | bytes 1769480 | tf_op jit(solution)/shard_map/ppermute | solution.py:269
  128.8 8.8 %collective-permute-start.22 = (bf16[192,1024]{1,0:T(8,128)(2,1)S(1)}, bf16[192,1024]{1,0:T(8,128)(2,1)S(1)}, u32[]{:S(2)}, u32[]{:S(2)}) collective-permute-start(bf16[192,1024]{1,0:T(8,128)(2,1)S(1)} %get-tuple-element.150), channel_id=1, source_target_pairs={{1,2},{2,1},{5,6},{6,5},{9,10},{10,9},{13,14},{14,13},{17,18},{18,... | collective-permute-start | bytes 1179656 | tf_op jit(solution)/shard_map/ppermute | solution.py:269
  129.5 8.2 %collective-permute-start.20 = (bf16[192,512]{1,0:T(8,128)(2,1)S(1)}, bf16[192,512]{1,0:T(8,128)(2,1)S(1)}, u32[]{:S(2)}, u32[]{:S(2)}) collective-permute-start(bf16[192,512]{1,0:T(8,128)(2,1)S(1)} %get-tuple-element.146), channel_id=1, source_target_pairs={{2,3},{1,0},{6,7},{5,4},{10,11},{9,8},{14,15},{13,12},{18,19},{17,... | collective-permute-start | bytes 589832 | tf_op jit(solution)/shard_map/ppermute | solution.py:269
  130.8 8.4 %collective-permute-start.19 = (bf16[192,512]{1,0:T(8,128)(2,1)S(1)}, bf16[192,512]{1,0:T(8,128)(2,1)S(1)}, u32[]{:S(2)}, u32[]{:S(2)}) collective-permute-start(bf16[192,512]{1,0:T(8,128)(2,1)S(1)} %get-tuple-element.145), channel_id=1, source_target_pairs={{2,3},{1,0},{6,7},{5,4},{10,11},{9,8},{14,15},{13,12},{18,19},{17,... | collective-permute-start | bytes 589832 | tf_op jit(solution)/shard_map/ppermute | solution.py:269
  132.3 5.4 %copy-start = (bf16[768,2048]{1,0:T(8,128)(2,1)S(1)}, bf16[768,2048]{1,0:T(8,128)(2,1)}, u32[]{:S(2)}) copy-start(bf16[768,2048]{1,0:T(8,128)(2,1)} %refs_4_.9) | copy-start | bytes 9437188
  140.1 7.0 %collective-permute-start.23 = (bf16[192,1024]{1,0:T(8,128)(2,1)S(1)}, bf16[192,1024]{1,0:T(8,128)(2,1)S(1)}, u32[]{:S(2)}, u32[]{:S(2)}) collective-permute-start(bf16[192,1024]{1,0:T(8,128)(2,1)S(1)} %get-tuple-element.162), channel_id=1, source_target_pairs={{1,2},{2,1},{5,6},{6,5},{9,10},{10,9},{13,14},{14,13},{17,18},{18,... | collective-permute-start | bytes 1179656 | tf_op jit(solution)/shard_map/ppermute | solution.py:269
  140.8 8.7 %collective-permute-start.25 = (bf16[192,512]{1,0:T(8,128)(2,1)S(1)}, bf16[192,512]{1,0:T(8,128)(2,1)S(1)}, u32[]{:S(2)}, u32[]{:S(2)}) collective-permute-start(bf16[192,512]{1,0:T(8,128)(2,1)S(1)} %get-tuple-element.165), channel_id=1, source_target_pairs={{2,3},{1,0},{6,7},{5,4},{10,11},{9,8},{14,15},{13,12},{18,19},{17,... | collective-permute-start | bytes 589832 | tf_op jit(solution)/shard_map/ppermute | solution.py:269
  147.2 9.7 %collective-permute-start.24 = (bf16[192,512]{1,0:T(8,128)(2,1)S(1)}, bf16[192,512]{1,0:T(8,128)(2,1)S(1)}, u32[]{:S(2)}, u32[]{:S(2)}) collective-permute-start(bf16[192,512]{1,0:T(8,128)(2,1)S(1)} %get-tuple-element.164), channel_id=1, source_target_pairs={{2,3},{1,0},{6,7},{5,4},{10,11},{9,8},{14,15},{13,12},{18,19},{17,... | collective-permute-start | bytes 589832 | tf_op jit(solution)/shard_map/ppermute | solution.py:269

commit v2 on v1

--- a/solution.py
+++ b/solution.py
@@ -14,16 +14,14 @@
 SMEM = pl.BlockSpec(memory_space=pltpu.SMEM)
 f32 = jnp.float32
 bf16 = jnp.bfloat16
-NT = (((1,), (1,)), ((), ()))
-TN = (((0,), (0,)), ((), ()))
 
 
 def params(mib=20):
     return pltpu.CompilerParams(vmem_limit_bytes=mib << 20)
 
 
-def cost(flops, nbytes):
-    return pl.CostEstimate(flops=1, bytes_accessed=1, transcendentals=0)
+def cost(word):
+    return pl.CostEstimate(flops=HEAVY.get(word, 1), bytes_accessed=1, transcendentals=0)
 
 
 def lanes(index, size):
@@ -143,13 +141,13 @@
         dact = None
         for j in range(per_column):
             k = table[per_column * h + j]
-            term = lax.dot_general(err[mine, lanes(rows_ref[k], blk)], down[k], NT, preferred_element_type=f32)
+            term = jnp.dot(err[mine, lanes(rows_ref[k], blk)], down[k], preferred_element_type=f32)
             dact = term if dact is None else dact + term
         s = slice(h * blk, (h + 1) * blk)
         dpre[mine, s] = (dact * fac[mine, s].astype(f32)).astype(bf16)
     for k in range(blocks):
         r = rows_ref[k]
-        acc[r] += lax.dot_general(dpre[mine, lanes(cols_ref[k], blk)], up[k], NT, preferred_element_type=f32)
+        acc[r] += jnp.dot(dpre[mine, lanes(cols_ref[k], blk)], up[k], preferred_element_type=f32)
     for b in range(acc.shape[0]):
         back[:, b * blk:(b + 1) * blk] = (acc[b] * scale_in).astype(bf16)
     out = shares_of(back, outs, sems.at[1])
@@ -216,6 +214,12 @@
     for b, c in enumerate(columns):
         copies[b].wait()
         tok_t[b] = tok[:, c].T
+
+
+def turn_weights_kernel(up, down, dep, also, up_t, down_t, token):
+    for k in range(up.shape[0]):
+        up_t[k] = up[k].T
+        down_t[k] = down[k].T
 
 
 def grad_kernel(scale, by_hidden, rows_ref, cols_ref, left, right, own, peer_hbm, dep, also, out_hbm, token,
@@ -316,7 +320,7 @@
             out_shape=(V(size, width), *held) + (like(size, part),) * direct + (token,),
             in_specs=specs, out_specs=(ANYV,) * (1 + len(held) + direct) + (ANY,),
             input_output_aliases=alias, scratch_shapes=scratch,
-            compiler_params=params(), name=f"forward_{c}", cost_estimate=cost(1, 1),
+            compiler_params=params(), name=f"forward_{c}", cost_estimate=cost(f"F{c}"),
         )(*a)
         if first:
             state.update(up=outs.pop(0), down=outs.pop(0))
@@ -335,7 +339,7 @@
             functools.partial(error_kernel, start, count), out_shape=(like(size, part), token),
             in_specs=[ANYV] * count + [ANY] * 3, out_specs=(ANYV, ANY),
             scratch_shapes=[V(size, part), pltpu.SemaphoreType.DMA],
-            compiler_params=params(), name=f"error_{c}", cost_estimate=cost(1, 1),
+            compiler_params=params(), name=f"error_{c}", cost_estimate=cost(f"S{c}"),
         )(part_of[c], *[got[c, i] for i in range(1, count)], in_hbm(targets), *after())
         state["dep"] = done
         got[c, 0] = e
@@ -347,7 +351,7 @@
         s, done = pl.pallas_call(
             add_kernel, out_shape=(like(size, width), token),
             in_specs=[ANYV, ANYV, ANY, ANY], out_specs=(ANYV, ANY),
-            compiler_params=params(), name=f"add_{c}_{j}", cost_estimate=cost(1, 1),
+            compiler_params=params(), name=f"add_{c}_{j}", cost_estimate=cost(f"A{c}{j}"),
         )(part_of[c], got[c, j - 1], *after())
         state["dep"] = done
         got[c, j] = hop(s, j)
@@ -360,7 +364,7 @@
         a = [block_rows, block_columns]
         for n in groups[c]:
             a += [got[n, 0] if ready else part_of[n]] + [got[n, j] for j in range(1, count)]
-        a += [in_hbm(targets), in_vmem(state["fac"]), *weights(), *after()]
+        a += [in_hbm(targets), in_vmem(state["fac"]), in_vmem(state["up_t"]), in_vmem(state["down_t"]), *after()]
         specs = [SMEM, SMEM] + [ANYV] * (count * len(groups[c])) + [ANY] + [ANYV] * 3 + [ANY] * 2
         alias = {}
         if not first:
@@ -376,7 +380,7 @@
             scratch_shapes=[V(size, width), pltpu.VMEM((model_blocks, size, blk), f32),
                             pltpu.SMEM((blocks,), jnp.int32), pltpu.SMEM((blocks // per_column,), jnp.int32),
                             pltpu.SemaphoreType.DMA((2,))],
-            compiler_params=params(), name=f"backward_{c}", cost_estimate=cost(1, 1),
+            compiler_params=params(), name=f"backward_{c}", cost_estimate=cost(f"B{c}"),
         )(*a)
         state.update(err=err, dpre=dpre, dep=done)
         back_of[c] = g
@@ -392,7 +396,7 @@
         s, done = pl.pallas_call(
             functools.partial(pass_on_kernel, j, count), out_shape=(like(size, wide), token),
             in_specs=[ANYV, ANYV, ANY, ANY], out_specs=(ANYV, ANY),
-            compiler_params=params(), name=f"pass_on_{c}_{j}", cost_estimate=cost(1, 1),
+            compiler_params=params(), name=f"pass_on_{c}_{j}", cost_estimate=cost(f"P{c}{j}"),
         )(back_of[c], gotg[c, j - 1], *after())
         state["dep"] = done
         gotg[c, j] = hop(s, j)
@@ -406,7 +410,7 @@
             in_specs=[ANYV] * count + [ANY] * 3, out_specs=(ANY, ANY),
             input_output_aliases={} if first else {count: 0},
             scratch_shapes=[V(size, part), pltpu.SemaphoreType.DMA],
-            compiler_params=params(), name=f"finish_{c}", cost_estimate=cost(size * width, 5 * size * width),
+            compiler_params=params(), name=f"finish_{c}", cost_estimate=cost(f"E{c}"),
         )(*a)
         state.update(out=o, dep=done)
 
@@ -415,9 +419,17 @@
         act_t, tok_t, done = pl.pallas_call(
             turn_kernel, out_shape=(turned, turned, token), in_specs=[ANYV] + [ANY] * 3, out_specs=(ANYV, ANYV, ANY),
             scratch_shapes=[V(tok_count, width), pltpu.SemaphoreType.DMA((model_blocks,))],
-            compiler_params=params(), name="turn", cost_estimate=cost(1, 1),
+            compiler_params=params(), name="turn", cost_estimate=cost("T0"),
         )(in_vmem(state["act"]), in_hbm(tokens), *after())
         state.update(act_t=act_t, tok_t=tok_t, dep=done)
+
+    def turn_weights():
+        W = V(blocks, blk, blk)
+        up_t, down_t, done = pl.pallas_call(
+            turn_weights_kernel, out_shape=(W, W, token), in_specs=[ANYV] * 2 + [ANY] * 2, out_specs=(ANYV, ANYV, ANY),
+            compiler_params=params(), name="turn_weights", cost_estimate=cost("W0"),
+        )(*weights(), *after())
+        state.update(up_t=up_t, down_t=down_t, dep=done)
 
     def grads(which):
         by_hidden = which == "down"
@@ -432,7 +444,7 @@
             scratch_shapes=[V(*own.shape), V(*own.shape),
                             pltpu.SMEM((blocks,), jnp.int32), pltpu.SMEM((blocks // per_column,), jnp.int32),
                             pltpu.SemaphoreType.DMA((2,))],
-            compiler_params=params(), name=f"grad_{which}", cost_estimate=cost(1, 1),
+            compiler_params=params(), name=f"grad_{which}", cost_estimate=cost("D0" if by_hidden else "U0"),
         )(block_rows, block_columns, in_vmem(left), in_vmem(right), in_vmem(own), in_hbm(peer), *after())
         new[which] = o
         state["dep"] = done
@@ -447,6 +459,8 @@
             error(c)
         elif what == "T":
             turn()
+        elif what == "W":
+            turn_weights()
         elif what == "X":
             state["also"] = (peer_up, peer_down)[c]
         elif what == "B":
@@ -461,8 +475,8 @@
 
 
 ORDER = (
-    "F0", "F1", "F2", "A02", "F3", "A12", "A03", "T0", "A22", "X0", "A13", "B0", "A32", "A23", "B1", "P02", "A33",
-    "B2", "X1", "P03", "P12", "B3", "P13", "P22", "D0", "P23", "E0", "E1", "P32", "U0", "P33", "E2", "E3",
+    "F0", "F1", "F2", "A02", "F3", "W0", "A12", "A03", "T0", "A22", "X0", "A13", "B0", "A32", "A23", "B1", "P02",
+    "A33", "B2", "P03", "P12", "X1", "B3", "E0", "P13", "P22", "D0", "P23", "U0", "E3", "E1", "E2",
 )
 
 
@@ -479,9 +493,10 @@
 
 
 SHARES = (192, 192, 192, 192)
+HEAVY = {"E1": 10000000000, "E3": 10000000000, "E2": 10000000000, "B1": 10000000000}
 GROUPS = ((0,), (1,), (2,), (3,))
 DIRECT_SUM = ()
-DIRECT_GRAD = ()
+DIRECT_GRAD = (3,)
 
 
 def solution(mesh):

time: 159 us -> 153 us (0.962)
  waiting for transfers between devices: 49.1 us -> 46.5 us
  starting transfers between devices: 54 us -> 52.1 us
    ppermute x24 -> x21, starting transfers between devices: 51 us -> 44 us  [hop(): return lax.ppermute(x, 'tensor', [(j - 1, j), (count - j, count - 1 - j)])]
    ppermute x24 -> x21, waiting for transfers between devices: 49.1 us -> 44.3 us  [hop(): return lax.ppermute(x, 'tensor', [(j - 1, j), (count - j, count - 1 - j)])]
    ppermute x0 -> x3, starting transfers between devices: none -> 4.45 us  [across(): return lax.ppermute(x, 'tensor', [(i, i ^ k) for i in range(count)])]
    ppermute x0 -> x3, waiting for transfers between devices: none -> 2.26 us  [across(): return lax.ppermute(x, 'tensor', [(i, i ^ k) for i in range(count)])]
  transfers between devices with their start and end apart: 26 -> 26, of which waited for: 11 -> 10; matrix products, arithmetic and copies ran while one was open for 0% -> 0% of each run, Pallas kernels for 29% -> 33%
where the time goes in v2:
time: 153 us; the launch traced here: 152 us
  starting transfers between devices  52.1 us (34%)
  Pallas kernels  50.5 us (33%)
  waiting for transfers between devices  46.5 us (30%)
    ppermute x21, waiting for transfers between devices, hop(): return lax.ppermute(x, 'tensor', [(j - 1, j), (count - j, count - 1 - j)])  44.3 us
    ppermute x21, starting transfers between devices, hop(): return lax.ppermute(x, 'tensor', [(j - 1, j), (count - j, count - 1 - j)])  44 us
    pallas_call x4, Pallas kernels, backward(): pl.pallas_call(functools.partial(backward_kernel, start, [chunks[n][1] fo...  17 us
    pallas_call x4, Pallas kernels, forward(): pl.pallas_call(functools.partial(forward_kernel, start, scale_in, scale_o...  14.8 us
    pallas_call x2, Pallas kernels, grads(): pl.pallas_call(functools.partial(grad_kernel, scale, by_hidden), out_shap...  10 us
    ppermute x3, starting transfers between devices, across(): return lax.ppermute(x, 'tensor', [(i, i ^ k) for i in range(count)])  4.45 us
    ppermute x2, starting transfers between devices, partner(): lax.ppermute(x, 'dp', [(i, i ^ 1 << level) for i in range(lax.axis_size('...  3.61 us
    pallas_call x4, Pallas kernels, finish(): pl.pallas_call(functools.partial(finish_kernel, start, count, c in direct...  3.19 us
  transfers between devices with their start and end apart: 26, of which 10 were waited for; matrix products, arithmetic and copies ran while one was open for 0% of the time, Pallas kernels for 33%

profile of v2, /device:TPU:0, one launch (start us, length us, event | category | flops | bytes accessed | tf_op | source)
XLA Modules:
  0.0 151.8 jit_solution(2617624532563147638)
XLA Ops:
  0.6 3.0 %collective-permute-start.7 = (bf16[16,256,256]{2,1,0:T(8,128)(2,1)}, bf16[16,256,256]{2,1,0:T(8,128)(2,1)S(1)}, u32[]{:S(2)}, u32[]{:S(2)}) collective-permute-start(bf16[16,256,256]{2,1,0:T(8,128)(2,1)} %bitcast.4), channel_id=1, source_target_pairs={{0,8},{4,12},{8,0},{12,4},{16,24},{20,28},{24,16},{28,20},{1,9},{5... | collective-permute-start | bytes 6291464 | tf_op jit(solution)/shard_map/ppermute | solution.py:279
  3.6 3.8 %forward_0.1 = (bf16[192,2048]{1,0:T(8,128)(2,1)S(1)}, bf16[768,2048]{1,0:T(8,128)(2,1)S(1)}, bf16[768,2048]{1,0:T(8,128)(2,1)S(1)}, bf16[16,256,256]{2,1,0:T(8,...) custom-call(s32[16]{0:T(128)} %rows_ref.19, s32[16]{0:T(128)} %cols_ref.19, ...), custom_call_target="tpu_custom_call" | custom-call | flops 1 | bytes 1 | tf_op jit(solution)/shard_map/forward_0/pallas_call | solution.py:318
  7.4 3.5 %collective-permute-start = (bf16[192,2048]{1,0:T(8,128)(2,1)S(1)}, bf16[192,2048]{1,0:T(8,128)(2,1)S(1)}, u32[]{:S(2)}, u32[]{:S(2)}) collective-permute-start(bf16[192,2048]{1,0:T(8,128)(2,1)S(1)} %get-tuple-element.90.a_ref.refs_0_), channel_id=1, source_target_pairs={{0,1},{3,2},{4,5},{7,6},{8,9},{11,10},{12,13},{15,14},{16,17},{19,... | collective-permute-start | bytes 2359304 | tf_op jit(solution)/shard_map/ppermute | solution.py:273
  11.0 3.7 %forward_1.1 = (bf16[192,2048]{1,0:T(8,128)(2,1)S(1)}, bf16[768,2048]{1,0:T(8,128)(2,1)S(1)}, bf16[768,2048]{1,0:T(8,128)(2,1)S(1)}, bf16[16,128]{1,0:T(8,128)(2,1)}) custom-call(s32[16]{0:T(128)S(1)} %copy-done.3, s32[16]{0:T(128)S(1)} %copy-done.4, bf16[768,2048]{1,0:T(8,128)(2,1)} %refs_4_.9, ...), custom_call_target="tpu_custom_call", output_to_operand_aliasing={{1}: (7, {}), {2}: (8, {})} | custom-call | flops 1 | bytes 1 | tf_op jit(solution)/shard_map/forward_1/pallas_call | solution.py:318
  14.6 1.3 collective-permute-start.2
  16.0 3.7 %forward_2.1 = (bf16[192,2048]{1,0:T(8,128)(2,1)S(1)}, bf16[768,2048]{1,0:T(8,128)(2,1)S(1)}, bf16[768,2048]{1,0:T(8,128)(2,1)S(1)}, bf16[16,128]{1,0:T(8,128)(2,1)}) custom-call(s32[16]{0:T(128)S(1)} %copy-done.3, s32[16]{0:T(128)S(1)} %copy-done.4, bf16[768,2048]{1,0:T(8,128)(2,1)} %refs_4_.9, ...), custom_call_target="tpu_custom_call", output_to_operand_aliasing={{1}: (7, {}), {2}: (8, {})} | custom-call | flops 1 | bytes 1 | tf_op jit(solution)/shard_map/forward_2/pallas_call | solution.py:318
  19.6 9.2 %collective-permute-done.b_ref.refs_1_ = bf16[192,2048]{1,0:T(8,128)(2,1)S(1)} collective-permute-done((bf16[192,2048]{1,0:T(8,128)(2,1)S(1)}, bf16[192,2048]{1,0:T(8,128)(2,1)S(1)}, u32[]{:S(2)}, u32[]{:S(2)}) %collective-permute-start) | collective-permute-done | bytes 786464 | tf_op jit(solution)/shard_map/ppermute | solution.py:273
  28.9 0.2 add_0_2.1
  29.0 0.7 collective-permute-start.1
  29.8 7.2 %collective-permute-start.6 = (bf16[192,2048]{1,0:T(8,128)(2,1)S(1)}, bf16[192,2048]{1,0:T(8,128)(2,1)S(1)}, u32[]{:S(2)}, u32[]{:S(2)}) collective-permute-start(bf16[192,2048]{1,0:T(8,128)(2,1)S(1)} %get-tuple-element.115.a_ref.refs_0_), channel_id=1, source_target_pairs={{0,1},{3,2},{4,5},{7,6},{8,9},{11,10},{12,13},{15,14},{16,17},{19,... | collective-permute-start | bytes 2359304 | tf_op jit(solution)/shard_map/ppermute | solution.py:273
  37.0 3.7 %forward_3.1 = (bf16[192,2048]{1,0:T(8,128)(2,1)S(1)}, bf16[768,2048]{1,0:T(8,128)(2,1)S(1)}, bf16[768,2048]{1,0:T(8,128)(2,1)S(1)}, bf16[16,128]{1,0:T(8,128)(2,1)}) custom-call(s32[16]{0:T(128)S(1)} %copy-done.3, s32[16]{0:T(128)S(1)} %copy-done.4, bf16[768,2048]{1,0:T(8,128)(2,1)} %refs_4_.9, ...), custom_call_target="tpu_custom_call", output_to_operand_aliasing={{1}: (7, {}), {2}: (8, {})} | custom-call | flops 1 | bytes 1 | tf_op jit(solution)/shard_map/forward_3/pallas_call | solution.py:318
  40.7 1.1 turn_weights.1
  41.8 3.9 %collective-permute-done.2.b_ref.refs_1_ = bf16[192,2048]{1,0:T(8,128)(2,1)S(1)} collective-permute-done((bf16[192,2048]{1,0:T(8,128)(2,1)S(1)}, bf16[192,2048]{1,0:T(8,128)(2,1)S(1)}, u32[]{:S(2)}, u32[]{:S(2)}) %collective-permute-start.2) | collective-permute-done | bytes 786464 | tf_op jit(solution)/shard_map/ppermute | solution.py:273
  45.7 0.2 add_1_2.1
  45.9 0.7 collective-permute-start.5
  46.6 0.2 add_0_3.1
  46.8 1.3 collective-permute-start.4
  48.1 7.5 %collective-permute-start.3 = (bf16[192,2048]{1,0:T(8,128)(2,1)S(1)}, bf16[192,2048]{1,0:T(8,128)(2,1)S(1)}, u32[]{:S(2)}, u32[]{:S(2)}) collective-permute-start(bf16[192,2048]{1,0:T(8,128)(2,1)S(1)} %get-tuple-element.109.a_ref.refs_0_), channel_id=1, source_target_pairs={{0,1},{3,2},{4,5},{7,6},{8,9},{11,10},{12,13},{15,14},{16,17},{19,... | collective-permute-start | bytes 2359304 | tf_op jit(solution)/shard_map/ppermute | solution.py:273
  55.6 2.4 %turn.1 = (bf16[8,256,768]{2,1,0:T(8,128)(2,1)S(1)}, bf16[8,256,768]{2,1,0:T(8,128)(2,1)S(1)}, bf16[16,128]{1,0:T(8,128)(2,1)}) custom-call(bf16[768,2048]{1,0:T(8,128)(2,1)S(1)} %get-tuple-element.101.act, bf16[768,2048]{1,0:T(8,128)(2,1)} %refs_4_.9, bf16[16,128]{1,0:T(8,128)(2,1)} %get-tuple-element.107.dep.also, bf16[16,128]{1,0:T(8,128)(2,1)} %get-tuple-element.107.dep.also), custom_call_target="tpu_custom_call" | custom-call | flops 1 | bytes 1 | tf_op jit(solution)/shard_map/turn/pallas_call | solution.py:419
  58.0 4.6 %collective-permute-done.6.b_ref.refs_1_ = bf16[192,2048]{1,0:T(8,128)(2,1)S(1)} collective-permute-done((bf16[192,2048]{1,0:T(8,128)(2,1)S(1)}, bf16[192,2048]{1,0:T(8,128)(2,1)S(1)}, u32[]{:S(2)}, u32[]{:S(2)}) %collective-permute-start.6) | collective-permute-done | bytes 786464 | tf_op jit(solution)/shard_map/ppermute | solution.py:273
  62.6 0.2 add_2_2.1
  62.7 0.7 collective-permute-start.11
  63.5 1.3 copy-done.6
  64.8 0.2 add_1_3.1
  65.0 1.3 collective-permute-start.10
  66.3 0.6 collective-permute-start.16
  66.9 1.0 collective-permute-done.4.refs_3_
  67.9 4.0 %backward_0.1 = (bf16[192,2048]{1,0:T(8,128)(2,1)S(1)}, bf16[192,1536]{1,0:T(8,128)(2,1)S(1)}, bf16[768,2048]{1,0:T(8,128)(2,1)S(1)}, bf16[768,2048]{1,0:T(8,128)(2,1)S(1)}, bf16[16,128]{1,0:T(8,128)(2,1)}) custom-call(s32[16]{0:T(128)S(1)} %copy-done.3, s32[16]{0:T(128)S(1)} %copy-done.4, bf16[192,2048]{1,0:T(8,128)(2,1)S(1)} %get-tuple-element.90.a_ref.refs_0_, ...), custom_call_target="tpu_custom_call" | custom-call | flops 1 | bytes 1 | tf_op jit(solution)/shard_map/backward_0/pallas_call | solution.py:375
  72.0 6.2 %collective-permute-start.9 = (bf16[192,1536]{1,0:T(8,128)(2,1)S(1)}, bf16[192,1536]{1,0:T(8,128)(2,1)S(1)}, u32[]{:S(2)}, u32[]{:S(2)}) collective-permute-start(bf16[192,1536]{1,0:T(8,128)(2,1)S(1)} %get-tuple-element.122), channel_id=1, source_target_pairs={{0,1},{3,2},{4,5},{7,6},{8,9},{11,10},{12,13},{15,14},{16,17},{19,... | collective-permute-start | bytes 1769480 | tf_op jit(solution)/shard_map/ppermute | solution.py:273
  78.2 1.2 collective-permute-done.3.b_ref.refs_1_
  79.4 0.2 add_3_2.1
  79.6 0.7 collective-permute-start.8
  80.3 0.2 add_2_3.1
  80.5 1.3 collective-permute-start.15
  81.8 5.6 %collective-permute-done.10.refs_3_ = bf16[192,2048]{1,0:T(8,128)(2,1)S(1)} collective-permute-done((bf16[192,2048]{1,0:T(8,128)(2,1)S(1)}, bf16[192,2048]{1,0:T(8,128)(2,1)S(1)}, u32[]{:S(2)}, u32[]{:S(2)}) %collective-permute-start.10) | collective-permute-done | bytes 786464 | tf_op jit(solution)/shard_map/ppermute | solution.py:273
  87.4 4.0 %backward_1.1 = (bf16[192,2048]{1,0:T(8,128)(2,1)S(1)}, bf16[192,1536]{1,0:T(8,128)(2,1)S(1)}, bf16[768,2048]{1,0:T(8,128)(2,1)S(1)}, bf16[768,2048]{1,0:T(8,128)(2,1)S(1)}, bf16[16,128]{1,0:T(8,128)(2,1)}) custom-call(s32[16]{0:T(128)S(1)} %copy-done.3, s32[16]{0:T(128)S(1)} %copy-done.4, ...), custom_call_target="tpu_custom_call", output_to_operand_aliasing={{2}: (12, {}), {3}: (13, {})} | custom-call | flops 10000000000 | bytes 1 | tf_op jit(solution)/shard_map/backward_1/pallas_call | solution.py:375
  91.4 1.7 %collective-permute-start.13 = (bf16[192,1536]{1,0:T(8,128)(2,1)S(1)}, bf16[192,1536]{1,0:T(8,128)(2,1)S(1)}, u32[]{:S(2)}, u32[]{:S(2)}) collective-permute-start(bf16[192,1536]{1,0:T(8,128)(2,1)S(1)} %get-tuple-element.133), channel_id=1, source_target_pairs={{0,1},{3,2},{4,5},{7,6},{8,9},{11,10},{12,13},{15,14},{16,17},{19,... | collective-permute-start | bytes 1769480 | tf_op jit(solution)/shard_map/ppermute | solution.py:273
  93.1 0.1 pass_on_0_2.1
  93.3 0.7 collective-permute-start.14
  94.0 0.2 add_3_3.1
  94.2 1.3 collective-permute-start.12
  95.5 10.1 %collective-permute-done.15.refs_3_ = bf16[192,2048]{1,0:T(8,128)(2,1)S(1)} collective-permute-done((bf16[192,2048]{1,0:T(8,128)(2,1)S(1)}, bf16[192,2048]{1,0:T(8,128)(2,1)S(1)}, u32[]{:S(2)}, u32[]{:S(2)}) %collective-permute-start.15) | collective-permute-done | bytes 786464 | tf_op jit(solution)/shard_map/ppermute | solution.py:273
  105.5 4.0 %backward_2.1 = (bf16[192,2048]{1,0:T(8,128)(2,1)S(1)}, bf16[192,1536]{1,0:T(8,128)(2,1)S(1)}, bf16[768,2048]{1,0:T(8,128)(2,1)S(1)}, bf16[768,2048]{1,0:T(8,128)(2,1)S(1)}, bf16[16,128]{1,0:T(8,128)(2,1)}) custom-call(s32[16]{0:T(128)S(1)} %copy-done.3, s32[16]{0:T(128)S(1)} %copy-done.4, ...), custom_call_target="tpu_custom_call", output_to_operand_aliasing={{2}: (12, {}), {3}: (13, {})} | custom-call | flops 1 | bytes 1 | tf_op jit(solution)/shard_map/backward_2/pallas_call | solution.py:375
  109.6 2.4 %collective-permute-start.17 = (bf16[192,1536]{1,0:T(8,128)(2,1)S(1)}, bf16[192,1536]{1,0:T(8,128)(2,1)S(1)}, u32[]{:S(2)}, u32[]{:S(2)}) collective-permute-start(bf16[192,1536]{1,0:T(8,128)(2,1)S(1)} %get-tuple-element.146), channel_id=1, source_target_pairs={{0,1},{3,2},{4,5},{7,6},{8,9},{11,10},{12,13},{15,14},{16,17},{19,... | collective-permute-start | bytes 1769480 | tf_op jit(solution)/shard_map/ppermute | solution.py:273
  112.1 0.1 pass_on_1_2.1
  112.2 0.7 collective-permute-start.18
  112.9 1.5 collective-permute-start.19
  114.4 7.5 %collective-permute-done.12.refs_3_ = bf16[192,2048]{1,0:T(8,128)(2,1)S(1)} collective-permute-done((bf16[192,2048]{1,0:T(8,128)(2,1)S(1)}, bf16[192,2048]{1,0:T(8,128)(2,1)S(1)}, u32[]{:S(2)}, u32[]{:S(2)}) %collective-permute-start.12) | collective-permute-done | bytes 786464 | tf_op jit(solution)/shard_map/ppermute | solution.py:273
  121.9 4.9 %backward_3.1 = (bf16[192,2048]{1,0:T(8,128)(2,1)S(1)}, bf16[16,128]{1,0:T(8,128)(2,1)}, bf16[768,2048]{1,0:T(8,128)(2,1)S(1)}, bf16[768,2048]{1,0:T(8,128)(2,1)...) custom-call(s32[16]{0:T(128)S(1)} %copy-done.3, ...), custom_call_target="tpu_custom_call", output_to_operand_aliasing={{2}: (12, {}), {3}: (13, {})} | custom-call | flops 1 | bytes 1 | tf_op jit(solution)/shard_map/backward_3/pallas_call | solution.py:375
  126.9 0.8 finish_0.1
  127.8 0.1 pass_on_2_2.1
  127.9 0.7 collective-permute-start.20
  128.6 1.3 collective-permute-start.23
  129.9 1.1 collective-permute-start.24
  131.0 2.1 %collective-permute-start.25 = (bf16[192,512]{1,0:T(8,128)(2,1)S(1)}, bf16[192,512]{1,0:T(8,128)(2,1)S(1)}, u32[]{:S(2)}, u32[]{:S(2)}) collective-permute-start(bf16[192,512]{1,0:T(8,128)(2,1)S(1)} %get-tuple-element.165), channel_id=1, source_target_pairs={{0,3},{1,2},{2,1},{3,0},{4,7},{5,6},{6,5},{7,4},{8,11},{9,10},{10,... | collective-permute-start | bytes 589832 | tf_op jit(solution)/shard_map/ppermute | solution.py:276
  133.1 1.3 collective-permute-start.22
  134.4 5.1 %grad_down.1 = (bf16[16,256,256]{2,1,0:T(8,128)(2,1)}, bf16[16,128]{1,0:T(8,128)(2,1)}) custom-call(s32[16]{0:T(128)S(1)} %copy-done.3, s32[16]{0:T(128)S(1)} %copy-done.4, bf16[8,256,768]{2,1,0:T(8,128)(2,1)S(1)} %copy-done.2, bf16[768,2048]{1,0:T(8,128)(2,1)S(1)} %get-tuple-element.154.right, bf16[16,256,256]{2,1,0:T(8,128)(2,1)S(1)} %get-tuple-element.89.down.own, ...), custom_call_target="tpu_custom_call" | custom-call | flops 1 | bytes 1 | tf_op jit(solution)/shard_map/grad_down/pallas_call | solution.py:441
  139.5 1.3 collective-permute-start.21
  140.8 4.9 %grad_up.1 = (bf16[16,256,256]{2,1,0:T(8,128)(2,1)}, bf16[16,128]{1,0:T(8,128)(2,1)}) custom-call(s32[16]{0:T(128)S(1)} %copy-done.3, s32[16]{0:T(128)S(1)} %copy-done.4, bf16[8,256,768]{2,1,0:T(8,128)(2,1)S(1)} %get-tuple-element.108.left, bf16[768,2048]{1,0:T(8,128)(2,1)S(1)} %get-tuple-element.144.right, ...), custom_call_target="tpu_custom_call" | custom-call | flops 1 | bytes 1 | tf_op jit(solution)/shard_map/grad_up/pallas_call | solution.py:441
  145.8 2.3 %collective-permute-done.24.refs_2_ = bf16[192,512]{1,0:T(8,128)(2,1)S(1)} collective-permute-done((bf16[192,512]{1,0:T(8,128)(2,1)S(1)}, bf16[192,512]{1,0:T(8,128)(2,1)S(1)}, u32[]{:S(2)}, u32[]{:S(2)}) %collective-permute-start.24) | collective-permute-done | bytes 196640 | tf_op jit(solution)/shard_map/ppermute | solution.py:276
  148.1 0.8 finish_3.1
  148.9 0.8 finish_1.1
  149.7 1.2 collective-permute-done.21.refs_3_
  150.8 0.8 finish_2.1
  (34 shorter events, 0.3 us)
Async XLA Ops:
  0.6 62.8 %collective-permute-start.7 = (bf16[16,256,256]{2,1,0:T(8,128)(2,1)}, bf16[16,256,256]{2,1,0:T(8,128)(2,1)S(1)}, u32[]{:S(2)}, u32[]{:S(2)}) collective-permute-start(bf16[16,256,256]{2,1,0:T(8,128)(2,1)} %bitcast.4), channel_id=1, source_target_pairs={{0,8},{4,12},{8,0},{12,4},{16,24},{20,28},{24,16},{28,20},{1,9},{5... | collective-permute-start | bytes 6291464 | tf_op jit(solution)/shard_map/ppermute | solution.py:279
  3.6 7.3 %copy-start.3 = (s32[16]{0:T(128)S(1)}, s32[16]{0:T(128)}, u32[]{:S(2)}) copy-start(s32[16]{0:T(128)} %rows_ref.19) | copy-start | bytes 196
  3.6 7.3 %copy-start.4 = (s32[16]{0:T(128)S(1)}, s32[16]{0:T(128)}, u32[]{:S(2)}) copy-start(s32[16]{0:T(128)} %cols_ref.19) | copy-start | bytes 196
  7.4 21.4 %collective-permute-start = (bf16[192,2048]{1,0:T(8,128)(2,1)S(1)}, bf16[192,2048]{1,0:T(8,128)(2,1)S(1)}, u32[]{:S(2)}, u32[]{:S(2)}) collective-permute-start(bf16[192,2048]{1,0:T(8,128)(2,1)S(1)} %get-tuple-element.90.a_ref.refs_0_), channel_id=1, source_target_pairs={{0,1},{3,2},{4,5},{7,6},{8,9},{11,10},{12,13},{15,14},{16,17},{19,... | collective-permute-start | bytes 2359304 | tf_op jit(solution)/shard_map/ppermute | solution.py:273
  14.6 31.1 %collective-permute-start.2 = (bf16[192,2048]{1,0:T(8,128)(2,1)S(1)}, bf16[192,2048]{1,0:T(8,128)(2,1)S(1)}, u32[]{:S(2)}, u32[]{:S(2)}) collective-permute-start(bf16[192,2048]{1,0:T(8,128)(2,1)S(1)} %get-tuple-element.103.a_ref.refs_0_), channel_id=1, source_target_pairs={{0,1},{3,2},{4,5},{7,6},{8,9},{11,10},{12,13},{15,14},{16,17},{19,... | collective-permute-start | bytes 2359304 | tf_op jit(solution)/shard_map/ppermute | solution.py:273
  29.0 17.6 %collective-permute-start.1 = (bf16[192,2048]{1,0:T(8,128)(2,1)S(1)}, bf16[192,2048]{1,0:T(8,128)(2,1)S(1)}, u32[]{:S(2)}, u32[]{:S(2)}) collective-permute-start(bf16[192,2048]{1,0:T(8,128)(2,1)S(1)} %get-tuple-element.102), channel_id=1, source_target_pairs={{1,2},{2,1},{5,6},{6,5},{9,10},{10,9},{13,14},{14,13},{17,18},{18,... | collective-permute-start | bytes 2359304 | tf_op jit(solution)/shard_map/ppermute | solution.py:273
  29.8 32.8 %collective-permute-start.6 = (bf16[192,2048]{1,0:T(8,128)(2,1)S(1)}, bf16[192,2048]{1,0:T(8,128)(2,1)S(1)}, u32[]{:S(2)}, u32[]{:S(2)}) collective-permute-start(bf16[192,2048]{1,0:T(8,128)(2,1)S(1)} %get-tuple-element.115.a_ref.refs_0_), channel_id=1, source_target_pairs={{0,1},{3,2},{4,5},{7,6},{8,9},{11,10},{12,13},{15,14},{16,17},{19,... | collective-permute-start | bytes 2359304 | tf_op jit(solution)/shard_map/ppermute | solution.py:273
  45.9 17.6 %collective-permute-start.5 = (bf16[192,2048]{1,0:T(8,128)(2,1)S(1)}, bf16[192,2048]{1,0:T(8,128)(2,1)S(1)}, u32[]{:S(2)}, u32[]{:S(2)}) collective-permute-start(bf16[192,2048]{1,0:T(8,128)(2,1)S(1)} %get-tuple-element.114), channel_id=1, source_target_pairs={{1,2},{2,1},{5,6},{6,5},{9,10},{10,9},{13,14},{14,13},{17,18},{18,... | collective-permute-start | bytes 2359304 | tf_op jit(solution)/shard_map/ppermute | solution.py:273
  46.8 21.1 %collective-permute-start.4 = (bf16[192,2048]{1,0:T(8,128)(2,1)S(1)}, bf16[192,2048]{1,0:T(8,128)(2,1)S(1)}, u32[]{:S(2)}, u32[]{:S(2)}) collective-permute-start(bf16[192,2048]{1,0:T(8,128)(2,1)S(1)} %get-tuple-element.110), channel_id=1, source_target_pairs={{2,3},{1,0},{6,7},{5,4},{10,11},{9,8},{14,15},{13,12},{18,19},{17,... | collective-permute-start | bytes 2359304 | tf_op jit(solution)/shard_map/ppermute | solution.py:273
  48.1 31.3 %collective-permute-start.3 = (bf16[192,2048]{1,0:T(8,128)(2,1)S(1)}, bf16[192,2048]{1,0:T(8,128)(2,1)S(1)}, u32[]{:S(2)}, u32[]{:S(2)}) collective-permute-start(bf16[192,2048]{1,0:T(8,128)(2,1)S(1)} %get-tuple-element.109.a_ref.refs_0_), channel_id=1, source_target_pairs={{0,1},{3,2},{4,5},{7,6},{8,9},{11,10},{12,13},{15,14},{16,17},{19,... | collective-permute-start | bytes 2359304 | tf_op jit(solution)/shard_map/ppermute | solution.py:273
  58.0 10.0 %copy-start.1 = (bf16[8,256,768]{2,1,0:T(8,128)(2,1)}, bf16[8,256,768]{2,1,0:T(8,128)(2,1)S(1)}, u32[]{:S(2)}) copy-start(bf16[8,256,768]{2,1,0:T(8,128)(2,1)S(1)} %get-tuple-element.153.left) | copy-start | bytes 9437188
  58.0 8.3 %copy-start.7 = (bf16[1,16,256,256]{3,2,1,0:T(8,128)(2,1)S(1)}, bf16[1,16,256,256]{3,2,1,0:T(8,128)(2,1)}, u32[]{:S(2)}) copy-start(bf16[1,16,256,256]{3,2,1,0:T(8,128)(2,1)} %param.9) | copy-start | bytes 6291460
  62.7 17.6 %collective-permute-start.11 = (bf16[192,2048]{1,0:T(8,128)(2,1)S(1)}, bf16[192,2048]{1,0:T(8,128)(2,1)S(1)}, u32[]{:S(2)}, u32[]{:S(2)}) collective-permute-start(bf16[192,2048]{1,0:T(8,128)(2,1)S(1)} %get-tuple-element.124), channel_id=1, source_target_pairs={{1,2},{2,1},{5,6},{6,5},{9,10},{10,9},{13,14},{14,13},{17,18},{18,... | collective-permute-start | bytes 2359304 | tf_op jit(solution)/shard_map/ppermute | solution.py:273
  63.5 1.3 copy-start.6
  65.0 22.4 %collective-permute-start.10 = (bf16[192,2048]{1,0:T(8,128)(2,1)S(1)}, bf16[192,2048]{1,0:T(8,128)(2,1)S(1)}, u32[]{:S(2)}, u32[]{:S(2)}) collective-permute-start(bf16[192,2048]{1,0:T(8,128)(2,1)S(1)} %get-tuple-element.123), channel_id=1, source_target_pairs={{2,3},{1,0},{6,7},{5,4},{10,11},{9,8},{14,15},{13,12},{18,19},{17,... | collective-permute-start | bytes 2359304 | tf_op jit(solution)/shard_map/ppermute | solution.py:273
  66.3 48.1 %collective-permute-start.16 = (bf16[16,256,256]{2,1,0:T(8,128)(2,1)S(1)}, bf16[16,256,256]{2,1,0:T(8,128)(2,1)S(1)}, u32[]{:S(2)}, u32[]{:S(2)}) collective-permute-start(bf16[16,256,256]{2,1,0:T(8,128)(2,1)S(1)} %bitcast.7), channel_id=1, source_target_pairs={{0,8},{4,12},{8,0},{12,4},{16,24},{20,28},{24,16},{28,20},{1,9},{5... | collective-permute-start | bytes 6291464 | tf_op jit(solution)/shard_map/ppermute | solution.py:279
  72.0 21.1 %collective-permute-start.9 = (bf16[192,1536]{1,0:T(8,128)(2,1)S(1)}, bf16[192,1536]{1,0:T(8,128)(2,1)S(1)}, u32[]{:S(2)}, u32[]{:S(2)}) collective-permute-start(bf16[192,1536]{1,0:T(8,128)(2,1)S(1)} %get-tuple-element.122), channel_id=1, source_target_pairs={{0,1},{3,2},{4,5},{7,6},{8,9},{11,10},{12,13},{15,14},{16,17},{19,... | collective-permute-start | bytes 1769480 | tf_op jit(solution)/shard_map/ppermute | solution.py:273
  79.6 14.4 %collective-permute-start.8 = (bf16[192,2048]{1,0:T(8,128)(2,1)S(1)}, bf16[192,2048]{1,0:T(8,128)(2,1)S(1)}, u32[]{:S(2)}, u32[]{:S(2)}) collective-permute-start(bf16[192,2048]{1,0:T(8,128)(2,1)S(1)} %get-tuple-element.120), channel_id=1, source_target_pairs={{1,2},{2,1},{5,6},{6,5},{9,10},{10,9},{13,14},{14,13},{17,18},{18,... | collective-permute-start | bytes 2359304 | tf_op jit(solution)/shard_map/ppermute | solution.py:273
  80.5 25.0 %collective-permute-start.15 = (bf16[192,2048]{1,0:T(8,128)(2,1)S(1)}, bf16[192,2048]{1,0:T(8,128)(2,1)S(1)}, u32[]{:S(2)}, u32[]{:S(2)}) collective-permute-start(bf16[192,2048]{1,0:T(8,128)(2,1)S(1)} %get-tuple-element.135), channel_id=1, source_target_pairs={{2,3},{1,0},{6,7},{5,4},{10,11},{9,8},{14,15},{13,12},{18,19},{17,... | collective-permute-start | bytes 2359304 | tf_op jit(solution)/shard_map/ppermute | solution.py:273
  91.4 20.7 %collective-permute-start.13 = (bf16[192,1536]{1,0:T(8,128)(2,1)S(1)}, bf16[192,1536]{1,0:T(8,128)(2,1)S(1)}, u32[]{:S(2)}, u32[]{:S(2)}) collective-permute-start(bf16[192,1536]{1,0:T(8,128)(2,1)S(1)} %get-tuple-element.133), channel_id=1, source_target_pairs={{0,1},{3,2},{4,5},{7,6},{8,9},{11,10},{12,13},{15,14},{16,17},{19,... | collective-permute-start | bytes 1769480 | tf_op jit(solution)/shard_map/ppermute | solution.py:273
  93.3 18.7 %collective-permute-start.14 = (bf16[192,1024]{1,0:T(8,128)(2,1)S(1)}, bf16[192,1024]{1,0:T(8,128)(2,1)S(1)}, u32[]{:S(2)}, u32[]{:S(2)}) collective-permute-start(bf16[192,1024]{1,0:T(8,128)(2,1)S(1)} %get-tuple-element.134), channel_id=1, source_target_pairs={{1,2},{2,1},{5,6},{6,5},{9,10},{10,9},{13,14},{14,13},{17,18},{18,... | collective-permute-start | bytes 1179656 | tf_op jit(solution)/shard_map/ppermute | solution.py:273
  94.2 27.8 %collective-permute-start.12 = (bf16[192,2048]{1,0:T(8,128)(2,1)S(1)}, bf16[192,2048]{1,0:T(8,128)(2,1)S(1)}, u32[]{:S(2)}, u32[]{:S(2)}) collective-permute-start(bf16[192,2048]{1,0:T(8,128)(2,1)S(1)} %get-tuple-element.131), channel_id=1, source_target_pairs={{2,3},{1,0},{6,7},{5,4},{10,11},{9,8},{14,15},{13,12},{18,19},{17,... | collective-permute-start | bytes 2359304 | tf_op jit(solution)/shard_map/ppermute | solution.py:273
  109.6 18.2 %collective-permute-start.17 = (bf16[192,1536]{1,0:T(8,128)(2,1)S(1)}, bf16[192,1536]{1,0:T(8,128)(2,1)S(1)}, u32[]{:S(2)}, u32[]{:S(2)}) collective-permute-start(bf16[192,1536]{1,0:T(8,128)(2,1)S(1)} %get-tuple-element.146), channel_id=1, source_target_pairs={{0,1},{3,2},{4,5},{7,6},{8,9},{11,10},{12,13},{15,14},{16,17},{19,... | collective-permute-start | bytes 1769480 | tf_op jit(solution)/shard_map/ppermute | solution.py:273
  112.2 15.5 %collective-permute-start.18 = (bf16[192,1024]{1,0:T(8,128)(2,1)S(1)}, bf16[192,1024]{1,0:T(8,128)(2,1)S(1)}, u32[]{:S(2)}, u32[]{:S(2)}) collective-permute-start(bf16[192,1024]{1,0:T(8,128)(2,1)S(1)} %get-tuple-element.147), channel_id=1, source_target_pairs={{1,2},{2,1},{5,6},{6,5},{9,10},{10,9},{13,14},{14,13},{17,18},{18,... | collective-permute-start | bytes 1179656 | tf_op jit(solution)/shard_map/ppermute | solution.py:273
  112.9 14.0 %collective-permute-start.19 = (bf16[192,512]{1,0:T(8,128)(2,1)S(1)}, bf16[192,512]{1,0:T(8,128)(2,1)S(1)}, u32[]{:S(2)}, u32[]{:S(2)}) collective-permute-start(bf16[192,512]{1,0:T(8,128)(2,1)S(1)} %get-tuple-element.148), channel_id=1, source_target_pairs={{2,3},{1,0},{6,7},{5,4},{10,11},{9,8},{14,15},{13,12},{18,19},{17,... | collective-permute-start | bytes 589832 | tf_op jit(solution)/shard_map/ppermute | solution.py:273
  114.4 7.5 %copy-start.5 = (bf16[16,256,256]{2,1,0:T(8,128)(2,1)}, bf16[16,256,256]{2,1,0:T(8,128)(2,1)S(1)}, u32[]{:S(2)}) copy-start(bf16[16,256,256]{2,1,0:T(8,128)(2,1)S(1)} %collective-permute-done.16.refs_9_.peer_hbm) | copy-start | bytes 6291460
  121.9 4.9 %copy-start = (bf16[768,2048]{1,0:T(8,128)(2,1)S(1)}, bf16[768,2048]{1,0:T(8,128)(2,1)}, u32[]{:S(2)}) copy-start(bf16[768,2048]{1,0:T(8,128)(2,1)} %refs_4_.9) | copy-start | bytes 9437188
  126.9 7.5 %copy-start.2 = (bf16[8,256,768]{2,1,0:T(8,128)(2,1)S(1)}, bf16[8,256,768]{2,1,0:T(8,128)(2,1)}, u32[]{:S(2)}) copy-start(bf16[8,256,768]{2,1,0:T(8,128)(2,1)} %copy-done.1) | copy-start | bytes 9437188
  127.9 11.6 %collective-permute-start.20 = (bf16[192,1024]{1,0:T(8,128)(2,1)S(1)}, bf16[192,1024]{1,0:T(8,128)(2,1)S(1)}, u32[]{:S(2)}, u32[]{:S(2)}) collective-permute-start(bf16[192,1024]{1,0:T(8,128)(2,1)S(1)} %get-tuple-element.152), channel_id=1, source_target_pairs={{1,2},{2,1},{5,6},{6,5},{9,10},{10,9},{13,14},{14,13},{17,18},{18,... | collective-permute-start | bytes 1179656 | tf_op jit(solution)/shard_map/ppermute | solution.py:273
  128.6 17.2 %collective-permute-start.23 = (bf16[192,512]{1,0:T(8,128)(2,1)S(1)}, bf16[192,512]{1,0:T(8,128)(2,1)S(1)}, u32[]{:S(2)}, u32[]{:S(2)}) collective-permute-start(bf16[192,512]{1,0:T(8,128)(2,1)S(1)} %get-tuple-element.163), channel_id=1, source_target_pairs={{0,1},{1,0},{2,3},{3,2},{4,5},{5,4},{6,7},{7,6},{8,9},{9,8},{10,11... | collective-permute-start | bytes 589832 | tf_op jit(solution)/shard_map/ppermute | solution.py:276
  129.9 18.2 %collective-permute-start.24 = (bf16[192,512]{1,0:T(8,128)(2,1)S(1)}, bf16[192,512]{1,0:T(8,128)(2,1)S(1)}, u32[]{:S(2)}, u32[]{:S(2)}) collective-permute-start(bf16[192,512]{1,0:T(8,128)(2,1)S(1)} %get-tuple-element.164), channel_id=1, source_target_pairs={{0,2},{1,3},{2,0},{3,1},{4,6},{5,7},{6,4},{7,5},{8,10},{9,11},{10,... | collective-permute-start | bytes 589832 | tf_op jit(solution)/shard_map/ppermute | solution.py:276
  131.0 17.1 %collective-permute-start.25 = (bf16[192,512]{1,0:T(8,128)(2,1)S(1)}, bf16[192,512]{1,0:T(8,128)(2,1)S(1)}, u32[]{:S(2)}, u32[]{:S(2)}) collective-permute-start(bf16[192,512]{1,0:T(8,128)(2,1)S(1)} %get-tuple-element.165), channel_id=1, source_target_pairs={{0,3},{1,2},{2,1},{3,0},{4,7},{5,6},{6,5},{7,4},{8,11},{9,10},{10,... | collective-permute-start | bytes 589832 | tf_op jit(solution)/shard_map/ppermute | solution.py:276
  133.1 15.8 %collective-permute-start.22 = (bf16[192,512]{1,0:T(8,128)(2,1)S(1)}, bf16[192,512]{1,0:T(8,128)(2,1)S(1)}, u32[]{:S(2)}, u32[]{:S(2)}) collective-permute-start(bf16[192,512]{1,0:T(8,128)(2,1)S(1)} %get-tuple-element.161), channel_id=1, source_target_pairs={{2,3},{1,0},{6,7},{5,4},{10,11},{9,8},{14,15},{13,12},{18,19},{17,... | collective-permute-start | bytes 589832 | tf_op jit(solution)/shard_map/ppermute | solution.py:273
  139.5 11.3 %collective-permute-start.21 = (bf16[192,512]{1,0:T(8,128)(2,1)S(1)}, bf16[192,512]{1,0:T(8,128)(2,1)S(1)}, u32[]{:S(2)}, u32[]{:S(2)}) collective-permute-start(bf16[192,512]{1,0:T(8,128)(2,1)S(1)} %get-tuple-element.160), channel_id=1, source_target_pairs={{2,3},{1,0},{6,7},{5,4},{10,11},{9,8},{14,15},{13,12},{18,19},{17,... | collective-permute-start | bytes 589832 | tf_op jit(solution)/shard_map/ppermute | solution.py:273
